TPU v7x, 32 devices: a whole 2x2x4 slice. The times are simulated.
32 devices in a mesh: slide: 2 (over y), row: 8 (over z, x), col: 2 (over core).
Axes of the slice: x: 2, y: 2, z: 4, core: 2. Of those that a mesh axis runs over, the one named last changes fastest.
Arguments:
- nodes: bfloat16 [16384, 512], P(('slide', 'row', 'col')), parts along dimension 0, may hold values from -6 to 6
- ln_gain: float32 [512], replicated, may hold values from 0.1 to 1.9
- w_query: bfloat16 [512, 512], replicated, may hold values from -0.25 to 0.25
- w_key: bfloat16 [512, 512], replicated, may hold values from -0.25 to 0.25
- w_value: bfloat16 [512, 512], replicated, may hold values from -0.25 to 0.25
- w_out: bfloat16 [512, 512], replicated, may hold values from -0.25 to 0.25
- agg_gain: float32 [512], replicated, may hold values from 0.1 to 1.9
- tile_weight: bfloat16 [16, 128, 128, 128], P(('slide', 'row'), 'col'), parts along dimension 0, may hold values from 0 to 2
- tile_src: int32 [16, 128], P(('slide', 'row'), 'col'), parts along dimension 0, may hold values from 0 to 7
- tile_dst: int32 [16, 128], P(('slide', 'row'), 'col'), parts along dimension 0, may hold values from 0 to 19, as said below
- tile_live: int32 [16, 2], P(('slide', 'row'), 'col'), parts along dimension 0, may hold values from 16 to 64, as said below
Outputs:
- updated: bfloat16 [16384, 512], P(('slide', 'row', 'col')), parts along dimension 0
There are 2 independent parts, one for each index of `slide`. A program takes and returns all parts, laid end to end along the dimension named above; an argument that names none is the same for every part. Nothing has to cross between parts.
Inputs may be any that keep to these rules, and one draw needn't show every extreme that they name: A tile on device row i targets device row i + tile_dst // 4 - 2, which always lies in the grid. `tile_live`: some device of each slide has all 64 tiles live.
All inputs are finite; a program needn't handle non-finite values.
Results may differ from a plain program's by a relative error of at most 0.006.
Values may be sent and summed in bfloat16 or wider, within the bound.
No kernel may reach another device: no remote copies, remote signals or barrier semaphores. Data moves between devices by JAX's collectives and lax.ppermute only.
A program may use at most 64 MiB of HBM per device.

v0:
```python
import math

import jax
import jax.numpy as jnp
from jax import lax
from jax.sharding import PartitionSpec as P

HEADS = 8
HALO = 2


epsilon_norm = 1e-05


def from_behind(block, axis, distance):
    devices = range(lax.axis_size(axis))
    route = [(i - distance, i) for i in devices if i - distance in devices]
    return lax.ppermute(block, axis, route)


def rms_scale(features, gain):
    features = features.astype(jnp.float32)
    scale = lax.rsqrt(jnp.mean(features * features, axis=-1, keepdims=True) + epsilon_norm)
    return features * scale * gain


def tile_messages(query_tiles, key_tiles, value_tiles, weights):
    tile_count, tile_rows, features = query_tiles.shape
    head_dim = features // HEADS
    queries_4d = query_tiles.reshape(tile_count, tile_rows, HEADS, head_dim)
    keys_4d = key_tiles.reshape(tile_count, tile_rows, HEADS, head_dim)
    values_4d = value_tiles.reshape(tile_count, tile_rows, HEADS, head_dim)
    scores = jnp.einsum(
        "tqhd,tkhd->thqk", queries_4d, keys_4d, preferred_element_type=jnp.float32
    ) * (1.0 / math.sqrt(head_dim))
    gate = (weights[:, None] * jax.nn.sigmoid(scores)).astype(jnp.bfloat16)
    merged = jnp.einsum("thqk,tkhd->tqhd", gate, values_4d, preferred_element_type=jnp.float32)
    return merged.reshape(tile_count, tile_rows, features)


def local(
    nodes,
    ln_gain,
    w_query,
    w_key,
    w_value,
    w_out,
    agg_gain,
    tile_weight,
    tile_src,
    tile_dst,
    tile_live,
):
    rows_dev, features = nodes.shape
    tile_rows = tile_weight.shape[-1]
    normed = rms_scale(nodes, ln_gain).astype(jnp.bfloat16)
    query = jnp.dot(normed, w_query, preferred_element_type=jnp.float32).astype(jnp.bfloat16)
    keys = jnp.dot(normed, w_key, preferred_element_type=jnp.float32).astype(jnp.bfloat16)
    values = jnp.dot(normed, w_value, preferred_element_type=jnp.float32).astype(jnp.bfloat16)
    keys_all, values_all = (
        lax.all_gather(keys, "col", axis=0, tiled=True),
        lax.all_gather(values, "col", axis=0, tiled=True),
    )
    key_blocks = keys_all.reshape(-1, tile_rows, features)
    value_blocks = values_all.reshape(-1, tile_rows, features)
    window_parts = []
    for offset in range(-HALO, HALO + 1):
        if offset == 0:
            window_parts.append(query)
        else:
            window_parts.append(from_behind(query, "row", -offset))
    query_blocks = jnp.concatenate(window_parts, axis=0).reshape(-1, tile_rows, features)
    window_slots = query_blocks.shape[0]
    tile_count = tile_src.shape[1]
    groups = tile_count // 8
    alive_all = (jnp.arange(tile_count, dtype=jnp.int32) < tile_live[0, 0]).astype(jnp.float32)
    inputs_all = (
        tile_weight[0].reshape(groups, 8, tile_rows, tile_rows),
        tile_src[0].reshape(groups, 8),
        tile_dst[0].reshape(groups, 8),
        alive_all.reshape(groups, 8),
    )
    slot_ids = jnp.arange(window_slots, dtype=jnp.int32)

    def visit(summed, inputs):
        weight, source, target, alive_mask = inputs
        weight = weight.astype(jnp.float32) * alive_mask[:, None, None]
        messages = tile_messages(
            jnp.take(query_blocks, target, axis=0),
            jnp.take(key_blocks, source, axis=0),
            jnp.take(value_blocks, source, axis=0),
            weight,
        )
        select = (target[:, None] == slot_ids[None, :]).astype(jnp.float32)
        return (
            summed + jnp.einsum("ts,tnd->snd", select, messages, precision=lax.Precision.HIGHEST),
            None,
        )

    summed = jnp.zeros((window_slots, tile_rows, features), jnp.float32)
    summed, _ = lax.scan(visit, summed, inputs_all)
    partial_value = summed.reshape(2 * HALO + 1, rows_dev, features)
    aggregate = partial_value[HALO]
    for offset in range(-HALO, HALO + 1):
        if offset != 0:
            aggregate = aggregate + from_behind(partial_value[HALO + offset], "row", offset)
    mixed = rms_scale(aggregate, agg_gain).astype(jnp.bfloat16)
    return (
        nodes.astype(jnp.float32) + jnp.dot(mixed, w_out, preferred_element_type=jnp.float32)
    ).astype(jnp.bfloat16)


def solution(mesh):
    return jax.shard_map(
        local,
        mesh=mesh,
        in_specs=(
            P(("slide", "row", "col"), None),
            P(),
            P(),
            P(),
            P(),
            P(),
            P(),
            P(("slide", "row"), "col", None, None),
            P(("slide", "row"), "col"),
            P(("slide", "row"), "col"),
            P(("slide", "row"), "col"),
        ),
        out_specs=P(("slide", "row", "col"), None),
        check_vma=False,
    )
```

profile of v0, /device:TPU:8, one launch (start us, length us, event | category | flops | bytes accessed | tf_op | source)
XLA Modules:
  0.0 333.5 jit_solution(16718330027264600189)
XLA Ops:
  8.0 2.4 convolution_convert_fusion
  11.0 3.5 %collective-permute-start = (bf16[512,512]{1,0:T(8,128)(2,1)S(1)}, bf16[512,512]{1,0:T(8,128)(2,1)S(1)}, u32[]{:S(2)}, u32[]{:S(2)}) collective-permute-start(bf16[512,512]{1,0:T(8,128)(2,1)S(1)} %convolution_convert_fusion.1), channel_id=1, source_target_pairs={{0,4},{2,6},{4,8},{6,10},{8,12},{10,14},{1,5},{3,7},{5,9},{7,11},{... | collective-permute-start | bytes 1572872 | tf_op jit(solution)/shard_map/ppermute | solution.py:18
  15.8 3.4 %collective-permute-start.1 = (bf16[512,512]{1,0:T(8,128)(2,1)S(1)}, bf16[512,512]{1,0:T(8,128)(2,1)S(1)}, u32[]{:S(2)}, u32[]{:S(2)}) collective-permute-start(bf16[512,512]{1,0:T(8,128)(2,1)S(1)} %convolution_convert_fusion.1), channel_id=1, source_target_pairs={{0,2},{2,4},{4,6},{6,8},{8,10},{10,12},{12,14},{1,3},{3,5},{5,7},{... | collective-permute-start | bytes 1572872 | tf_op jit(solution)/shard_map/ppermute | solution.py:18
  19.2 3.3 %collective-permute-start.2 = (bf16[512,512]{1,0:T(8,128)(2,1)S(1)}, bf16[512,512]{1,0:T(8,128)(2,1)S(1)}, u32[]{:S(2)}, u32[]{:S(2)}) collective-permute-start(bf16[512,512]{1,0:T(8,128)(2,1)S(1)} %convolution_convert_fusion.1), channel_id=1, source_target_pairs={{2,0},{4,2},{6,4},{8,6},{10,8},{12,10},{14,12},{3,1},{5,3},{7,5},{... | collective-permute-start | bytes 1572872 | tf_op jit(solution)/shard_map/ppermute | solution.py:18
  27.9 13.5 %collective-permute-done.1 = bf16[512,512]{1,0:T(8,128)(2,1)S(1)} collective-permute-done((bf16[512,512]{1,0:T(8,128)(2,1)S(1)}, bf16[512,512]{1,0:T(8,128)(2,1)S(1)}, u32[]{:S(2)}, u32[]{:S(2)}) %collective-permute-start.1) | collective-permute-done | bytes 524320 | tf_op jit(solution)/shard_map/ppermute | solution.py:18
  43.0 2.4 collective-permute-done.2
  47.4 216.5 %while.11 = (s32[]{:T(128)}, f32[20,128,512]{2,0,1:T(8,128)}, s32[8,8]{1,0:T(8,128)S(1)}, s32[8,8]{1,0:T(8,128)S(1)}, bf16[8,128,512]{2,1,0:T(8,128)(2,1)}, /*in...) while((s32[]{:T(128)}, f32[20,128,512]{2,0,1:T(8,128)}, ...), condition=%wide.region_2.4_spmd.clone, body=%wide.region_1.3_spmd.clone.sunk | while | flops 405014816 | bytes 52699872 | solution.py:101
  48.6 2.4 gather_fusion.2
  56.3 2.4 copy.33
  60.0 5.5 %fusion.58 = f32[8,8,64,128]{3,2,1,0:T(8,128)} fusion(bf16[8,128,8,64]{1,3,2,0:T(8,128)(2,1)} %bitcast.80, bf16[8,128,8,64]{1,3,2,0:T(8,128)(2,1)} %bitcast.81, f32[8,128,128]{2,1,0:T(8,128)S(1)} %convert_multiply_fusion.4, bf16[8,128,8,64]{1,3,2,0:T(8,128)(2,1)S(1)} %bitcast.79, pred[8]{0:T(512)(128)(4,1)S(1)} %get-tuple-element.189), kind=kOutput, calls=%fused_computation.6.clone.1 | convolution fusion | flops 275251200 | bytes 5767176 | tf_op jit(solution)/shard_map/while/body/eval_jaxpr/thqk,tkhd->tqhd/dot_general | solution.py:37
  65.5 2.2 copy.36
  67.8 5.0 %select_add_fusion.2 = f32[20,128,512]{2,0,1:T(8,128)} fusion(f32[20,128,512]{2,0,1:T(8,128)} %get-tuple-element.203, pred[]{:T(512)S(6)} %compare.3, f32[8,128,512]{2,0,1:T(8,128)S(1)} %copy.36, s32[8]{0:T(128)S(1)} %get-tuple-element.190), kind=kOutput, calls=%fused_computation.4.clone.1 | convolution fusion | flops 128450720 | bytes 12582945 | tf_op jit(solution)/shard_map/while/body/eval_jaxpr/ts,tnd->snd/dot_general | solution.py:96
  74.0 2.4 gather_fusion.2
  81.7 2.4 copy.33
  85.4 5.5 %fusion.58 = f32[8,8,64,128]{3,2,1,0:T(8,128)} fusion(bf16[8,128,8,64]{1,3,2,0:T(8,128)(2,1)} %bitcast.80, bf16[8,128,8,64]{1,3,2,0:T(8,128)(2,1)} %bitcast.81, f32[8,128,128]{2,1,0:T(8,128)S(1)} %convert_multiply_fusion.4, bf16[8,128,8,64]{1,3,2,0:T(8,128)(2,1)S(1)} %bitcast.79, pred[8]{0:T(512)(128)(4,1)S(1)} %get-tuple-element.189), kind=kOutput, calls=%fused_computation.6.clone.1 | convolution fusion | flops 275251200 | bytes 5767176 | tf_op jit(solution)/shard_map/while/body/eval_jaxpr/thqk,tkhd->tqhd/dot_general | solution.py:37
  91.0 2.2 copy.36
  93.2 6.9 %select_add_fusion.2 = f32[20,128,512]{2,0,1:T(8,128)} fusion(f32[20,128,512]{2,0,1:T(8,128)} %get-tuple-element.203, pred[]{:T(512)S(6)} %compare.3, f32[8,128,512]{2,0,1:T(8,128)S(1)} %copy.36, s32[8]{0:T(128)S(1)} %get-tuple-element.190), kind=kOutput, calls=%fused_computation.4.clone.1 | convolution fusion | flops 128450720 | bytes 12582945 | tf_op jit(solution)/shard_map/while/body/eval_jaxpr/ts,tnd->snd/dot_general | solution.py:96
  101.3 2.4 gather_fusion.2
  109.0 2.4 copy.33
  112.7 5.5 %fusion.58 = f32[8,8,64,128]{3,2,1,0:T(8,128)} fusion(bf16[8,128,8,64]{1,3,2,0:T(8,128)(2,1)} %bitcast.80, bf16[8,128,8,64]{1,3,2,0:T(8,128)(2,1)} %bitcast.81, f32[8,128,128]{2,1,0:T(8,128)S(1)} %convert_multiply_fusion.4, bf16[8,128,8,64]{1,3,2,0:T(8,128)(2,1)S(1)} %bitcast.79, pred[8]{0:T(512)(128)(4,1)S(1)} %get-tuple-element.189), kind=kOutput, calls=%fused_computation.6.clone.1 | convolution fusion | flops 275251200 | bytes 5767176 | tf_op jit(solution)/shard_map/while/body/eval_jaxpr/thqk,tkhd->tqhd/dot_general | solution.py:37
  118.2 2.2 copy.36
  120.5 6.9 %select_add_fusion.2 = f32[20,128,512]{2,0,1:T(8,128)} fusion(f32[20,128,512]{2,0,1:T(8,128)} %get-tuple-element.203, pred[]{:T(512)S(6)} %compare.3, f32[8,128,512]{2,0,1:T(8,128)S(1)} %copy.36, s32[8]{0:T(128)S(1)} %get-tuple-element.190), kind=kOutput, calls=%fused_computation.4.clone.1 | convolution fusion | flops 128450720 | bytes 12582945 | tf_op jit(solution)/shard_map/while/body/eval_jaxpr/ts,tnd->snd/dot_general | solution.py:96
  128.6 2.4 gather_fusion.2
  136.3 2.4 copy.33
  140.0 5.5 %fusion.58 = f32[8,8,64,128]{3,2,1,0:T(8,128)} fusion(bf16[8,128,8,64]{1,3,2,0:T(8,128)(2,1)} %bitcast.80, bf16[8,128,8,64]{1,3,2,0:T(8,128)(2,1)} %bitcast.81, f32[8,128,128]{2,1,0:T(8,128)S(1)} %convert_multiply_fusion.4, bf16[8,128,8,64]{1,3,2,0:T(8,128)(2,1)S(1)} %bitcast.79, pred[8]{0:T(512)(128)(4,1)S(1)} %get-tuple-element.189), kind=kOutput, calls=%fused_computation.6.clone.1 | convolution fusion | flops 275251200 | bytes 5767176 | tf_op jit(solution)/shard_map/while/body/eval_jaxpr/thqk,tkhd->tqhd/dot_general | solution.py:37
  147.8 6.9 %select_add_fusion.2 = f32[20,128,512]{2,0,1:T(8,128)} fusion(f32[20,128,512]{2,0,1:T(8,128)} %get-tuple-element.203, pred[]{:T(512)S(6)} %compare.3, f32[8,128,512]{2,0,1:T(8,128)S(1)} %copy.36, s32[8]{0:T(128)S(1)} %get-tuple-element.190), kind=kOutput, calls=%fused_computation.4.clone.1 | convolution fusion | flops 128450720 | bytes 12582945 | tf_op jit(solution)/shard_map/while/body/eval_jaxpr/ts,tnd->snd/dot_general | solution.py:96
  155.9 2.4 gather_fusion.2
  163.6 2.4 copy.33
  167.3 5.5 %fusion.58 = f32[8,8,64,128]{3,2,1,0:T(8,128)} fusion(bf16[8,128,8,64]{1,3,2,0:T(8,128)(2,1)} %bitcast.80, bf16[8,128,8,64]{1,3,2,0:T(8,128)(2,1)} %bitcast.81, f32[8,128,128]{2,1,0:T(8,128)S(1)} %convert_multiply_fusion.4, bf16[8,128,8,64]{1,3,2,0:T(8,128)(2,1)S(1)} %bitcast.79, pred[8]{0:T(512)(128)(4,1)S(1)} %get-tuple-element.189), kind=kOutput, calls=%fused_computation.6.clone.1 | convolution fusion | flops 275251200 | bytes 5767176 | tf_op jit(solution)/shard_map/while/body/eval_jaxpr/thqk,tkhd->tqhd/dot_general | solution.py:37
  175.1 6.9 %select_add_fusion.2 = f32[20,128,512]{2,0,1:T(8,128)} fusion(f32[20,128,512]{2,0,1:T(8,128)} %get-tuple-element.203, pred[]{:T(512)S(6)} %compare.3, f32[8,128,512]{2,0,1:T(8,128)S(1)} %copy.36, s32[8]{0:T(128)S(1)} %get-tuple-element.190), kind=kOutput, calls=%fused_computation.4.clone.1 | convolution fusion | flops 128450720 | bytes 12582945 | tf_op jit(solution)/shard_map/while/body/eval_jaxpr/ts,tnd->snd/dot_general | solution.py:96
  183.2 2.4 gather_fusion.2
  190.9 2.4 copy.33
  194.6 5.5 %fusion.58 = f32[8,8,64,128]{3,2,1,0:T(8,128)} fusion(bf16[8,128,8,64]{1,3,2,0:T(8,128)(2,1)} %bitcast.80, bf16[8,128,8,64]{1,3,2,0:T(8,128)(2,1)} %bitcast.81, f32[8,128,128]{2,1,0:T(8,128)S(1)} %convert_multiply_fusion.4, bf16[8,128,8,64]{1,3,2,0:T(8,128)(2,1)S(1)} %bitcast.79, pred[8]{0:T(512)(128)(4,1)S(1)} %get-tuple-element.189), kind=kOutput, calls=%fused_computation.6.clone.1 | convolution fusion | flops 275251200 | bytes 5767176 | tf_op jit(solution)/shard_map/while/body/eval_jaxpr/thqk,tkhd->tqhd/dot_general | solution.py:37
  202.4 6.9 %select_add_fusion.2 = f32[20,128,512]{2,0,1:T(8,128)} fusion(f32[20,128,512]{2,0,1:T(8,128)} %get-tuple-element.203, pred[]{:T(512)S(6)} %compare.3, f32[8,128,512]{2,0,1:T(8,128)S(1)} %copy.36, s32[8]{0:T(128)S(1)} %get-tuple-element.190), kind=kOutput, calls=%fused_computation.4.clone.1 | convolution fusion | flops 128450720 | bytes 12582945 | tf_op jit(solution)/shard_map/while/body/eval_jaxpr/ts,tnd->snd/dot_general | solution.py:96
  210.5 2.4 gather_fusion.2
  218.2 2.4 copy.33
  221.9 5.5 %fusion.58 = f32[8,8,64,128]{3,2,1,0:T(8,128)} fusion(bf16[8,128,8,64]{1,3,2,0:T(8,128)(2,1)} %bitcast.80, bf16[8,128,8,64]{1,3,2,0:T(8,128)(2,1)} %bitcast.81, f32[8,128,128]{2,1,0:T(8,128)S(1)} %convert_multiply_fusion.4, bf16[8,128,8,64]{1,3,2,0:T(8,128)(2,1)S(1)} %bitcast.79, pred[8]{0:T(512)(128)(4,1)S(1)} %get-tuple-element.189), kind=kOutput, calls=%fused_computation.6.clone.1 | convolution fusion | flops 275251200 | bytes 5767176 | tf_op jit(solution)/shard_map/while/body/eval_jaxpr/thqk,tkhd->tqhd/dot_general | solution.py:37
  229.7 6.9 %select_add_fusion.2 = f32[20,128,512]{2,0,1:T(8,128)} fusion(f32[20,128,512]{2,0,1:T(8,128)} %get-tuple-element.203, pred[]{:T(512)S(6)} %compare.3, f32[8,128,512]{2,0,1:T(8,128)S(1)} %copy.36, s32[8]{0:T(128)S(1)} %get-tuple-element.190), kind=kOutput, calls=%fused_computation.4.clone.1 | convolution fusion | flops 128450720 | bytes 12582945 | tf_op jit(solution)/shard_map/while/body/eval_jaxpr/ts,tnd->snd/dot_general | solution.py:96
  237.8 2.4 gather_fusion.2
  245.5 2.4 copy.33
  249.2 5.5 %fusion.58 = f32[8,8,64,128]{3,2,1,0:T(8,128)} fusion(bf16[8,128,8,64]{1,3,2,0:T(8,128)(2,1)} %bitcast.80, bf16[8,128,8,64]{1,3,2,0:T(8,128)(2,1)} %bitcast.81, f32[8,128,128]{2,1,0:T(8,128)S(1)} %convert_multiply_fusion.4, bf16[8,128,8,64]{1,3,2,0:T(8,128)(2,1)S(1)} %bitcast.79, pred[8]{0:T(512)(128)(4,1)S(1)} %get-tuple-element.189), kind=kOutput, calls=%fused_computation.6.clone.1 | convolution fusion | flops 275251200 | bytes 5767176 | tf_op jit(solution)/shard_map/while/body/eval_jaxpr/thqk,tkhd->tqhd/dot_general | solution.py:37
  257.0 6.9 %select_add_fusion.2 = f32[20,128,512]{2,0,1:T(8,128)} fusion(f32[20,128,512]{2,0,1:T(8,128)} %get-tuple-element.203, pred[]{:T(512)S(6)} %compare.3, f32[8,128,512]{2,0,1:T(8,128)S(1)} %copy.36, s32[8]{0:T(128)S(1)} %get-tuple-element.190), kind=kOutput, calls=%fused_computation.4.clone.1 | convolution fusion | flops 128450720 | bytes 12582945 | tf_op jit(solution)/shard_map/while/body/eval_jaxpr/ts,tnd->snd/dot_general | solution.py:96
  263.8 5.8 %copy.24 = f32[20,128,512]{2,1,0:T(8,128)S(1)} copy(f32[20,128,512]{2,0,1:T(8,128)} %get-tuple-element.58) | data formatting | bytes 10485760 | tf_op jit(solution)/shard_map/while | solution.py:101
  270.4 3.3 collective-permute-start.7
  275.7 4.8 %collective-permute-start.5 = (f32[512,512]{1,0:T(8,128)S(1)}, f32[512,512]{1,0:T(8,128)S(1)}, u32[]{:S(2)}, u32[]{:S(2)}) collective-permute-start(f32[512,512]{1,0:T(8,128)S(1)} %bitcast.83), channel_id=1, source_target_pairs={{2,0},{4,2},{6,4},{8,6},{10,8},{12,10},{14,12},{3,1},{5,3},{7,5},{... | collective-permute-start | bytes 3145736 | tf_op jit(solution)/shard_map/ppermute | solution.py:18
  282.5 13.3 %collective-permute-done.7 = f32[512,512]{1,0:T(8,128)S(1)} collective-permute-done((f32[512,512]{1,0:T(8,128)S(1)}, f32[512,512]{1,0:T(8,128)S(1)}, u32[]{:S(2)}, u32[]{:S(2)}) %collective-permute-start.7) | collective-permute-done | bytes 1048608 | tf_op jit(solution)/shard_map/ppermute | solution.py:18
  295.8 23.4 %collective-permute-done.6 = f32[512,512]{1,0:T(8,128)S(1)} collective-permute-done((f32[512,512]{1,0:T(8,128)S(1)}, f32[512,512]{1,0:T(8,128)S(1)}, u32[]{:S(2)}, u32[]{:S(2)}) %collective-permute-start.6) | collective-permute-done | bytes 1048608 | tf_op jit(solution)/shard_map/ppermute | solution.py:18
  319.1 4.1 %collective-permute-done.5 = f32[512,512]{1,0:T(8,128)S(1)} collective-permute-done((f32[512,512]{1,0:T(8,128)S(1)}, f32[512,512]{1,0:T(8,128)S(1)}, u32[]{:S(2)}, u32[]{:S(2)}) %collective-permute-start.5) | collective-permute-done | bytes 1048608 | tf_op jit(solution)/shard_map/ppermute | solution.py:18
  (193 shorter events, 93.2 us)
Async XLA Ops:
  6.5 1.4 copy-start
  6.5 3.9 %copy-start.4 = (bf16[512,512]{1,0:T(8,128)(2,1)S(1)}, bf16[512,512]{1,0:T(8,128)(2,1)}, u32[]{:S(2)}) copy-start(bf16[512,512]{1,0:T(8,128)(2,1)} %param.15) | copy-start | bytes 1572868
  6.5 3.9 %copy-start.10 = (f32[512]{0:T(512)S(1)}, f32[512]{0:T(512)}, u32[]{:S(2)}) copy-start(f32[512]{0:T(512)} %param.16) | copy-start | bytes 6148
  6.5 3.9 %copy-start.8 = (bf16[512,512]{1,0:T(8,128)(2,1)S(1)}, bf16[512,512]{1,0:T(8,128)(2,1)}, u32[]{:S(2)}) copy-start(bf16[512,512]{1,0:T(8,128)(2,1)} %param.17) | copy-start | bytes 1572868
  6.5 7.9 %copy-start.9 = (bf16[512,512]{1,0:T(8,128)(2,1)S(1)}, bf16[512,512]{1,0:T(8,128)(2,1)}, u32[]{:S(2)}) copy-start(bf16[512,512]{1,0:T(8,128)(2,1)} %param.19) | copy-start | bytes 1572868
  6.5 40.8 %all-gather.5.cloned.1.call-start = ((), (), s32[]{:S(2)}) async-start(), calls=%async_computation.1 | async-start | bytes 1572864 | tf_op jit(solution)/shard_map/all_gather | solution.py:61
  10.3 15.3 %copy-start.11 = (s32[1,64]{1,0:T(1,128)S(1)}, s32[1,64]{1,0:T(1,128)}, u32[]{:S(2)}) copy-start(s32[1,64]{1,0:T(1,128)} %param.23) | copy-start | bytes 772
  10.3 15.9 %copy-start.12 = (s32[1,64]{1,0:T(1,128)S(1)}, s32[1,64]{1,0:T(1,128)}, u32[]{:S(2)}) copy-start(s32[1,64]{1,0:T(1,128)} %param.24) | copy-start | bytes 772
  10.4 37.0 %all-gather.3.cloned.1.call-start = ((), (), s32[]{:S(2)}) async-start(), calls=%async_computation | async-start | bytes 1572864 | tf_op jit(solution)/shard_map/all_gather | solution.py:62
  11.0 16.1 %collective-permute-start = (bf16[512,512]{1,0:T(8,128)(2,1)S(1)}, bf16[512,512]{1,0:T(8,128)(2,1)S(1)}, u32[]{:S(2)}, u32[]{:S(2)}) collective-permute-start(bf16[512,512]{1,0:T(8,128)(2,1)S(1)} %convolution_convert_fusion.1), channel_id=1, source_target_pairs={{0,4},{2,6},{4,8},{6,10},{8,12},{10,14},{1,5},{3,7},{5,9},{7,11},{... | collective-permute-start | bytes 1572872 | tf_op jit(solution)/shard_map/ppermute | solution.py:18
  15.8 25.5 %collective-permute-start.1 = (bf16[512,512]{1,0:T(8,128)(2,1)S(1)}, bf16[512,512]{1,0:T(8,128)(2,1)S(1)}, u32[]{:S(2)}, u32[]{:S(2)}) collective-permute-start(bf16[512,512]{1,0:T(8,128)(2,1)S(1)} %convolution_convert_fusion.1), channel_id=1, source_target_pairs={{0,2},{2,4},{4,6},{6,8},{8,10},{10,12},{12,14},{1,3},{3,5},{5,7},{... | collective-permute-start | bytes 1572872 | tf_op jit(solution)/shard_map/ppermute | solution.py:18
  19.2 26.2 %collective-permute-start.2 = (bf16[512,512]{1,0:T(8,128)(2,1)S(1)}, bf16[512,512]{1,0:T(8,128)(2,1)S(1)}, u32[]{:S(2)}, u32[]{:S(2)}) collective-permute-start(bf16[512,512]{1,0:T(8,128)(2,1)S(1)} %convolution_convert_fusion.1), channel_id=1, source_target_pairs={{2,0},{4,2},{6,4},{8,6},{10,8},{12,10},{14,12},{3,1},{5,3},{7,5},{... | collective-permute-start | bytes 1572872 | tf_op jit(solution)/shard_map/ppermute | solution.py:18
  22.6 23.9 %collective-permute-start.3 = (bf16[512,512]{1,0:T(8,128)(2,1)S(1)}, bf16[512,512]{1,0:T(8,128)(2,1)S(1)}, u32[]{:S(2)}, u32[]{:S(2)}) collective-permute-start(bf16[512,512]{1,0:T(8,128)(2,1)S(1)} %convolution_convert_fusion.1), channel_id=1, source_target_pairs={{4,0},{6,2},{8,4},{10,6},{12,8},{14,10},{5,1},{7,3},{9,5},{11,7},{... | collective-permute-start | bytes 1572872 | tf_op jit(solution)/shard_map/ppermute | solution.py:18
  47.4 4.9 %copy-start.2 = (bf16[8,128,512]{2,1,0:T(8,128)(2,1)S(1)}, bf16[8,128,512]{2,1,0:T(8,128)(2,1)}, u32[]{:S(2)}) copy-start(bf16[8,128,512]{2,1,0:T(8,128)(2,1)} %get-tuple-element.217) | copy-start | bytes 3145732 | tf_op jit(solution)/shard_map/while
  56.3 2.4 copy-start.1
  56.3 3.7 %copy-start.3 = (bf16[8,128,512]{1,2,0:T(8,128)(2,1)S(1)}, bf16[8,128,512]{1,2,0:T(8,128)(2,1)}, u32[]{:S(2)}) copy-start(bf16[8,128,512]{1,2,0:T(8,128)(2,1)} %copy.35) | copy-start | bytes 3145732 | tf_op jit(solution)/shard_map/while
  72.8 4.9 %copy-start.2 = (bf16[8,128,512]{2,1,0:T(8,128)(2,1)S(1)}, bf16[8,128,512]{2,1,0:T(8,128)(2,1)}, u32[]{:S(2)}) copy-start(bf16[8,128,512]{2,1,0:T(8,128)(2,1)} %get-tuple-element.217) | copy-start | bytes 3145732 | tf_op jit(solution)/shard_map/while
  81.7 2.4 copy-start.1
  81.7 3.7 %copy-start.3 = (bf16[8,128,512]{1,2,0:T(8,128)(2,1)S(1)}, bf16[8,128,512]{1,2,0:T(8,128)(2,1)}, u32[]{:S(2)}) copy-start(bf16[8,128,512]{1,2,0:T(8,128)(2,1)} %copy.35) | copy-start | bytes 3145732 | tf_op jit(solution)/shard_map/while
  100.1 4.9 %copy-start.2 = (bf16[8,128,512]{2,1,0:T(8,128)(2,1)S(1)}, bf16[8,128,512]{2,1,0:T(8,128)(2,1)}, u32[]{:S(2)}) copy-start(bf16[8,128,512]{2,1,0:T(8,128)(2,1)} %get-tuple-element.217) | copy-start | bytes 3145732 | tf_op jit(solution)/shard_map/while
  109.0 2.4 copy-start.1
  109.0 3.7 %copy-start.3 = (bf16[8,128,512]{1,2,0:T(8,128)(2,1)S(1)}, bf16[8,128,512]{1,2,0:T(8,128)(2,1)}, u32[]{:S(2)}) copy-start(bf16[8,128,512]{1,2,0:T(8,128)(2,1)} %copy.35) | copy-start | bytes 3145732 | tf_op jit(solution)/shard_map/while
  127.4 4.9 %copy-start.2 = (bf16[8,128,512]{2,1,0:T(8,128)(2,1)S(1)}, bf16[8,128,512]{2,1,0:T(8,128)(2,1)}, u32[]{:S(2)}) copy-start(bf16[8,128,512]{2,1,0:T(8,128)(2,1)} %get-tuple-element.217) | copy-start | bytes 3145732 | tf_op jit(solution)/shard_map/while
  136.3 2.4 copy-start.1
  136.3 3.7 %copy-start.3 = (bf16[8,128,512]{1,2,0:T(8,128)(2,1)S(1)}, bf16[8,128,512]{1,2,0:T(8,128)(2,1)}, u32[]{:S(2)}) copy-start(bf16[8,128,512]{1,2,0:T(8,128)(2,1)} %copy.35) | copy-start | bytes 3145732 | tf_op jit(solution)/shard_map/while
  154.7 4.9 %copy-start.2 = (bf16[8,128,512]{2,1,0:T(8,128)(2,1)S(1)}, bf16[8,128,512]{2,1,0:T(8,128)(2,1)}, u32[]{:S(2)}) copy-start(bf16[8,128,512]{2,1,0:T(8,128)(2,1)} %get-tuple-element.217) | copy-start | bytes 3145732 | tf_op jit(solution)/shard_map/while
  163.6 2.4 copy-start.1
  163.6 3.7 %copy-start.3 = (bf16[8,128,512]{1,2,0:T(8,128)(2,1)S(1)}, bf16[8,128,512]{1,2,0:T(8,128)(2,1)}, u32[]{:S(2)}) copy-start(bf16[8,128,512]{1,2,0:T(8,128)(2,1)} %copy.35) | copy-start | bytes 3145732 | tf_op jit(solution)/shard_map/while
  182.0 4.9 %copy-start.2 = (bf16[8,128,512]{2,1,0:T(8,128)(2,1)S(1)}, bf16[8,128,512]{2,1,0:T(8,128)(2,1)}, u32[]{:S(2)}) copy-start(bf16[8,128,512]{2,1,0:T(8,128)(2,1)} %get-tuple-element.217) | copy-start | bytes 3145732 | tf_op jit(solution)/shard_map/while
  190.9 2.4 copy-start.1
  190.9 3.7 %copy-start.3 = (bf16[8,128,512]{1,2,0:T(8,128)(2,1)S(1)}, bf16[8,128,512]{1,2,0:T(8,128)(2,1)}, u32[]{:S(2)}) copy-start(bf16[8,128,512]{1,2,0:T(8,128)(2,1)} %copy.35) | copy-start | bytes 3145732 | tf_op jit(solution)/shard_map/while
  209.3 4.9 %copy-start.2 = (bf16[8,128,512]{2,1,0:T(8,128)(2,1)S(1)}, bf16[8,128,512]{2,1,0:T(8,128)(2,1)}, u32[]{:S(2)}) copy-start(bf16[8,128,512]{2,1,0:T(8,128)(2,1)} %get-tuple-element.217) | copy-start | bytes 3145732 | tf_op jit(solution)/shard_map/while
  218.2 2.4 copy-start.1
  218.2 3.7 %copy-start.3 = (bf16[8,128,512]{1,2,0:T(8,128)(2,1)S(1)}, bf16[8,128,512]{1,2,0:T(8,128)(2,1)}, u32[]{:S(2)}) copy-start(bf16[8,128,512]{1,2,0:T(8,128)(2,1)} %copy.35) | copy-start | bytes 3145732 | tf_op jit(solution)/shard_map/while
  236.6 4.9 %copy-start.2 = (bf16[8,128,512]{2,1,0:T(8,128)(2,1)S(1)}, bf16[8,128,512]{2,1,0:T(8,128)(2,1)}, u32[]{:S(2)}) copy-start(bf16[8,128,512]{2,1,0:T(8,128)(2,1)} %get-tuple-element.217) | copy-start | bytes 3145732 | tf_op jit(solution)/shard_map/while
  245.5 2.4 copy-start.1
  245.5 3.7 %copy-start.3 = (bf16[8,128,512]{1,2,0:T(8,128)(2,1)S(1)}, bf16[8,128,512]{1,2,0:T(8,128)(2,1)}, u32[]{:S(2)}) copy-start(bf16[8,128,512]{1,2,0:T(8,128)(2,1)} %copy.35) | copy-start | bytes 3145732 | tf_op jit(solution)/shard_map/while
  270.4 25.4 %collective-permute-start.7 = (f32[512,512]{1,0:T(8,128)S(1)}, f32[512,512]{1,0:T(8,128)S(1)}, u32[]{:S(2)}, u32[]{:S(2)}) collective-permute-start(f32[512,512]{1,0:T(8,128)S(1)} %bitcast.85), channel_id=1, source_target_pairs={{0,4},{2,6},{4,8},{6,10},{8,12},{10,14},{1,5},{3,7},{5,9},{7,11},{... | collective-permute-start | bytes 3145736 | tf_op jit(solution)/shard_map/ppermute | solution.py:18
  273.8 45.4 %collective-permute-start.6 = (f32[512,512]{1,0:T(8,128)S(1)}, f32[512,512]{1,0:T(8,128)S(1)}, u32[]{:S(2)}, u32[]{:S(2)}) collective-permute-start(f32[512,512]{1,0:T(8,128)S(1)} %bitcast.84), channel_id=1, source_target_pairs={{0,2},{2,4},{4,6},{6,8},{8,10},{10,12},{12,14},{1,3},{3,5},{5,7},{... | collective-permute-start | bytes 3145736 | tf_op jit(solution)/shard_map/ppermute | solution.py:18
  275.7 47.5 %collective-permute-start.5 = (f32[512,512]{1,0:T(8,128)S(1)}, f32[512,512]{1,0:T(8,128)S(1)}, u32[]{:S(2)}, u32[]{:S(2)}) collective-permute-start(f32[512,512]{1,0:T(8,128)S(1)} %bitcast.83), channel_id=1, source_target_pairs={{2,0},{4,2},{6,4},{8,6},{10,8},{12,10},{14,12},{3,1},{5,3},{7,5},{... | collective-permute-start | bytes 3145736 | tf_op jit(solution)/shard_map/ppermute | solution.py:18
  280.5 43.6 %collective-permute-start.4 = (f32[512,512]{1,0:T(8,128)S(1)}, f32[512,512]{1,0:T(8,128)S(1)}, u32[]{:S(2)}, u32[]{:S(2)}) collective-permute-start(f32[512,512]{1,0:T(8,128)S(1)} %bitcast.82), channel_id=1, source_target_pairs={{4,0},{6,2},{8,4},{10,6},{12,8},{14,10},{5,1},{7,3},{9,5},{11,7},{... | collective-permute-start | bytes 3145736 | tf_op jit(solution)/shard_map/ppermute | solution.py:18
  324.2 1.0 copy-start.5
  324.2 1.2 copy-start.6
  324.2 1.2 copy-start.7
Sparse Core Ops, SparseCore 0:
  10.5 10.4 all-gather.4
  22.5 10.1 all-gather.2
where the time goes:
time: 338 us; the launch traced here: 333 us
  local copies, waits for them, and re-layouts  109 us (32%)
  matrix products  103 us (30%)
  waiting for transfers between devices  57.8 us (17%)
  other arithmetic  24.6 us (7%)
  starting transfers between devices  24.2 us (7%)
  between operations  14.2 us (4%)
    ppermute x8, waiting for transfers between devices, from_behind(): return lax.ppermute(block, axis, route)  57.7 us
    dot_general x8, matrix products, visit(): jnp.einsum('ts,tnd->snd', select, messages, precision=lax.Precision.HIGHEST)  53.2 us
    dot_general x8, matrix products, tile_messages(): jnp.einsum('thqk,tkhd->tqhd', gate, values_4d, preferred_element_type=jnp...  44.1 us
    gather x16, local copies, waits for them, and re-layouts, visit(): jnp.take(query_blocks, target, axis=0)  29.3 us
    ppermute x8, starting transfers between devices, from_behind(): return lax.ppermute(block, axis, route)  24.1 us
    select_n x8, local copies, waits for them, and re-layouts, visit(): jnp.take(value_blocks, source, axis=0)  19.4 us
    reshape x8, local copies, waits for them, and re-layouts, tile_messages(): return merged.reshape(tile_count, tile_rows, features)  18 us
    gather x8, local copies, waits for them, and re-layouts, visit(): jnp.take(key_blocks, source, axis=0)  14.7 us
  transfers between devices with their start and end apart: 10, of which 7 were waited for; matrix products, arithmetic and copies ran while one was open for 2% of the time, Pallas kernels for 0%

commit v1 on v0

v1 whole, which is shorter than its diff:
```python
import functools

import jax
import jax.numpy as jnp
from jax import lax
from jax.experimental import pallas as pl
from jax.experimental.pallas import tpu as pltpu
from jax.sharding import PartitionSpec as P

HEADS = 8
HALO = 2
UNROLL = 4
EPSILON = 1e-05
BF16 = jnp.bfloat16
F32 = jnp.float32
VMEM = pl.BlockSpec(memory_space=pltpu.VMEM)
SMEM = pl.BlockSpec(memory_space=pltpu.SMEM)


def along(block, axis, distance):
    count = lax.axis_size(axis)
    route = [(i, i + distance) for i in range(count) if 0 <= i + distance < count]
    return lax.ppermute(block, axis, route)


def swap(block, axis, first):
    count = lax.axis_size(axis)
    pairs = [(i, i + 1) for i in range(first, count - 1, 2)]
    return lax.ppermute(block, axis, pairs + [(j, i) for i, j in pairs])


def rms_scale(features, gain):
    features = features.astype(F32)
    scale = lax.rsqrt(jnp.mean(features * features, axis=-1, keepdims=True) + EPSILON)
    return features * scale * gain


def project(normed, weight_ref):
    return jnp.dot(normed, weight_ref[...], preferred_element_type=F32).astype(BF16)


def split_heads(block):
    lane = lax.broadcasted_iota(jnp.int32, block.shape, 1)
    first = lane < block.shape[1] // 2
    zero = jnp.zeros_like(block)
    return jnp.concatenate([jnp.where(first, block, zero), jnp.where(first, zero, block)], axis=0)


def store_queries(query, query_ref):
    query = query * BF16(1.0 / 16.0)
    rows = query_ref.shape[1]
    for block in range(query_ref.shape[0]):
        query_ref[block] = query[block * rows : (block + 1) * rows]


def visit_tiles(code, src_ref, dst_ref, live_ref, weight_ref, query_ref, key_ref, value_ref, acc_ref, list_ref):
    blocks = query_ref.shape[0]
    pairs = key_ref.shape[1]
    wide = key_ref.shape[3]
    acc_ref[...] = jnp.zeros_like(acc_ref)

    def collect(tile, found):
        list_ref[found] = tile
        return found + (dst_ref[0, tile] // blocks == code).astype(jnp.int32)

    found = lax.fori_loop(0, live_ref[0, 0], collect, 0)
    for extra in range(UNROLL):
        list_ref[found + extra] = 0

    def step(index, carry):
        tiles, gates = [], []
        for u in range(UNROLL):
            place = index * UNROLL + u
            tile = list_ref[place]
            source, target = src_ref[0, tile], dst_ref[0, tile] % blocks
            half = jnp.where(place < found, 0.5, 0.0)
            weight = (weight_ref[tile].astype(F32) * half).astype(BF16)
            weight = jnp.concatenate([weight, weight], axis=1)
            tiles.append((source, target))
            gate = []
            for pair in range(pairs):
                scores = lax.dot_general(
                    query_ref[target, :, pair * wide : (pair + 1) * wide],
                    key_ref[source, pair],
                    (((1,), (1,)), ((), ())),
                    preferred_element_type=F32,
                )
                gate.append(jnp.tanh(scores.astype(BF16)) * weight + weight)
            gates.append(gate)
        sums = [
            [jnp.dot(gate[pair], value_ref[source, pair], preferred_element_type=F32) for pair in range(pairs)]
            for (source, _), gate in zip(tiles, gates)
        ]
        for (_, target), total in zip(tiles, sums):
            for pair in range(pairs):
                acc_ref[target, :, pair * wide : (pair + 1) * wide] += total[pair]
        return carry

    lax.fori_loop(0, pl.cdiv(found, UNROLL), step, 0)


def pack_heads(full, packed_ref, base):
    rows = packed_ref.shape[2] // 2
    wide = packed_ref.shape[3]
    for block in range(full.shape[0] // rows):
        for pair in range(packed_ref.shape[1]):
            packed_ref[base + block, pair] = split_heads(
                full[block * rows : (block + 1) * rows, pair * wide : (pair + 1) * wide]
            )


def own_kernel(
    src_ref, dst_ref, live_ref, nodes_ref, other_ref, gain_ref, wq_ref, wk_ref, wv_ref, weight_ref,
    out_ref, key_ref, value_ref, query_ref, list_ref,
):
    me = lax.axis_index("col")
    blocks = out_ref.shape[0]
    normed = rms_scale(nodes_ref[...], gain_ref[...]).astype(BF16)
    store_queries(project(normed, wq_ref), query_ref)
    pack_heads(project(normed, wk_ref), key_ref, me * blocks)
    pack_heads(project(normed, wv_ref), value_ref, me * blocks)
    normed = rms_scale(other_ref[...], gain_ref[...]).astype(BF16)
    pack_heads(project(normed, wk_ref), key_ref, (1 - me) * blocks)
    pack_heads(project(normed, wv_ref), value_ref, (1 - me) * blocks)
    visit_tiles(
        HALO, src_ref, dst_ref, live_ref, weight_ref, query_ref, key_ref, value_ref, out_ref, list_ref
    )


def far_kernel(
    places, src_ref, dst_ref, live_ref, gain_ref, wq_ref, weight_ref, key_ref, value_ref, *refs
):
    count = len(places)
    node_refs, out_refs = refs[:count], refs[count : 2 * count]
    query_ref, acc_ref, list_ref = refs[2 * count :]
    odd = lax.axis_index("row") % 2
    for place, nodes_ref, out_ref in zip(places, node_refs, out_refs):
        code = HALO + (place if isinstance(place, int) else jnp.where(odd == place[0], 1, -1))
        store_queries(project(rms_scale(nodes_ref[...], gain_ref[...]).astype(BF16), wq_ref), query_ref)
        visit_tiles(
            code, src_ref, dst_ref, live_ref, weight_ref, query_ref, key_ref, value_ref, acc_ref, list_ref
        )
        for block in range(acc_ref.shape[0]):
            rows = acc_ref.shape[1]
            out_ref[block * rows : (block + 1) * rows] = acc_ref[block].astype(BF16)


def last_kernel(nodes_ref, gain_ref, w_out_ref, own_ref, a_ref, b_ref, c_ref, d_ref, out_ref):
    aggregate = own_ref[...].reshape(a_ref.shape) + a_ref[...].astype(F32) + b_ref[...].astype(F32)
    aggregate = aggregate + c_ref[...].astype(F32) + d_ref[...].astype(F32)
    mixed = rms_scale(aggregate, gain_ref[...]).astype(BF16)
    update = jnp.dot(mixed, w_out_ref[...], preferred_element_type=F32)
    out_ref[...] = (nodes_ref[...].astype(F32) + update).astype(BF16)


def local(nodes, ln_gain, w_query, w_key, w_value, w_out, agg_gain, tile_weight, tile_src, tile_dst, tile_live):
    rows_dev, features = nodes.shape
    tile_count, tile_rows = tile_weight.shape[1], tile_weight.shape[-1]
    blocks = rows_dev // tile_rows
    pairs = HEADS // 2
    wide = features // pairs
    sources = lax.axis_size("col") * blocks
    gain = ln_gain.reshape(1, features)
    weight = tile_weight[0]
    params = pltpu.CompilerParams(vmem_limit_bytes=40 << 20)

    def cost(groups):
        tile_flops = 4 * tile_rows * tile_rows * features * tile_count // 5
        return pl.CostEstimate(
            flops=groups * (4 * tile_flops + 2 * rows_dev * features * features),
            bytes_accessed=8 << 20,
            transcendentals=groups * HEADS * tile_rows * tile_rows * tile_count // 5,
        )

    query_scratch = pltpu.VMEM((blocks, tile_rows, features), BF16)
    list_scratch = pltpu.SMEM((tile_count + UNROLL,), jnp.int32)
    packed = jax.ShapeDtypeStruct((sources, pairs, 2 * tile_rows, wide), BF16)
    partial_f32 = jax.ShapeDtypeStruct((blocks, tile_rows, features), F32)
    partial_bf16 = jax.ShapeDtypeStruct((rows_dev, features), BF16)

    other = lax.ppermute(nodes, "col", [(0, 1), (1, 0)])
    near = swap(nodes, "row", 0)
    above = along(nodes, "row", -HALO)
    below = along(nodes, "row", HALO)
    diagonal = swap(nodes, "row", 1)

    own, keys, values = pl.pallas_call(
        own_kernel,
        out_shape=(partial_f32, packed, packed),
        in_specs=[SMEM] * 3 + [VMEM] * 7,
        out_specs=(VMEM, VMEM, VMEM),
        scratch_shapes=[query_scratch, list_scratch],
        compiler_params=params,
        cost_estimate=cost(1),
        name="own_tiles",
    )(tile_src, tile_dst, tile_live, nodes, other, gain, w_query, w_key, w_value, weight)

    def far(name, places, blocks_in):
        return pl.pallas_call(
            functools.partial(far_kernel, places),
            out_shape=(partial_bf16,) * len(places),
            in_specs=[SMEM] * 3 + [VMEM] * (5 + len(places)),
            out_specs=(VMEM,) * len(places),
            scratch_shapes=[query_scratch, pltpu.VMEM((blocks, tile_rows, features), F32), list_scratch],
            compiler_params=params,
            cost_estimate=cost(len(places)),
            name=name,
        )(tile_src, tile_dst, tile_live, gain, w_query, weight, keys, values, *blocks_in)

    near_part, above_part, below_part = far("near_tiles", ((0,), HALO, -HALO), (near, above, below))
    near_back = swap(near_part, "row", 0)
    above_back = along(above_part, "row", HALO)
    below_back = along(below_part, "row", -HALO)
    (diagonal_part,) = far("diagonal_tiles", ((1,),), (diagonal,))
    diagonal_back = swap(diagonal_part, "row", 1)

    return pl.pallas_call(
        last_kernel,
        out_shape=jax.ShapeDtypeStruct((rows_dev, features), BF16),
        in_specs=[VMEM] * 8,
        out_specs=VMEM,
        compiler_params=params,
        cost_estimate=pl.CostEstimate(
            flops=2 * rows_dev * features * features, bytes_accessed=4 << 20, transcendentals=0
        ),
        name="mix",
    )(nodes, agg_gain.reshape(1, features), w_out, own, near_back, above_back, below_back, diagonal_back)


def solution(mesh):
    return jax.shard_map(
        local,
        mesh=mesh,
        in_specs=(
            P(("slide", "row", "col"), None),
            P(),
            P(),
            P(),
            P(),
            P(),
            P(),
            P(("slide", "row"), "col", None, None),
            P(("slide", "row"), "col"),
            P(("slide", "row"), "col"),
            P(("slide", "row"), "col"),
        ),
        out_specs=P(("slide", "row", "col"), None),
        check_vma=False,
    )
```

time: 338 us -> 68.7 us (0.20)
  the two profiles are of different devices: /device:TPU:8 before, /device:TPU:6 now
where the time goes in v1:
time: 68.7 us; the launch traced here: 67.8 us
  starting transfers between devices  26.6 us (39%)
  Pallas kernels  20.4 us (30%)
  waiting for transfers between devices  12.2 us (18%)
  local copies, waits for them, and re-layouts  7.77 us (11%)
  between operations  0.84 us (1%)
    pallas_call x2, Pallas kernels, far(): pl.pallas_call(functools.partial(far_kernel, places), out_shape=(partial_...  14.2 us
    ppermute x4, starting transfers between devices, swap(): return lax.ppermute(block, axis, pairs + [(j, i) for i, j in pairs])  13.9 us
    ppermute x4, starting transfers between devices, along(): return lax.ppermute(block, axis, route)  12.7 us
    ppermute x4, waiting for transfers between devices, swap(): return lax.ppermute(block, axis, pairs + [(j, i) for i, j in pairs])  11.6 us
    unnamed x26, local copies, waits for them, and re-layouts  7.77 us
    pallas_call x1, Pallas kernels, local(): pl.pallas_call(own_kernel, out_shape=(partial_f32, packed, packed), in_sp...  4.62 us
    pallas_call x1, Pallas kernels, local(): pl.pallas_call(last_kernel, out_shape=jax.ShapeDtypeStruct((rows_dev, fea...  1.55 us
  transfers between devices with their start and end apart: 9, of which 2 were waited for; matrix products, arithmetic and copies ran while one was open for 0% of the time, Pallas kernels for 28%

profile of v1, /device:TPU:6, one launch (start us, length us, event | category | flops | bytes accessed | tf_op | source)
XLA Modules:
  0.0 67.8 jit_solution(13913703199506485306)
XLA Ops:
  0.0 0.0 collective-permute-start
  0.0 0.5 collective-permute-start.1
  0.5 1.3 %collective-permute-start.2 = (bf16[512,512]{1,0:T(8,128)(2,1)}, bf16[512,512]{1,0:T(8,128)(2,1)S(1)}, u32[]{:S(2)}, u32[]{:S(2)}) collective-permute-start(bf16[512,512]{1,0:T(8,128)(2,1)} %nodes_ref.3), channel_id=1, source_target_pairs={{4,0},{6,2},{8,4},{10,6},{12,8},{14,10},{5,1},{7,3},{9,5},{11,7},{... | collective-permute-start | bytes 1572872 | tf_op jit(solution)/shard_map/ppermute | solution.py:23
  1.8 4.6 %collective-permute-start.3 = (bf16[512,512]{1,0:T(8,128)(2,1)}, bf16[512,512]{1,0:T(8,128)(2,1)S(1)}, u32[]{:S(2)}, u32[]{:S(2)}) collective-permute-start(bf16[512,512]{1,0:T(8,128)(2,1)} %nodes_ref.3), channel_id=1, source_target_pairs={{0,4},{2,6},{4,8},{6,10},{8,12},{10,14},{1,5},{3,7},{5,9},{7,11},{... | collective-permute-start | bytes 1572872 | tf_op jit(solution)/shard_map/ppermute | solution.py:23
  6.4 4.4 %collective-permute-start.7 = (bf16[512,512]{1,0:T(8,128)(2,1)}, bf16[512,512]{1,0:T(8,128)(2,1)S(1)}, u32[]{:S(2)}, u32[]{:S(2)}) collective-permute-start(bf16[512,512]{1,0:T(8,128)(2,1)} %nodes_ref.3), channel_id=1, source_target_pairs={{2,4},{6,8},{10,12},{4,2},{8,6},{12,10},{3,5},{7,9},{11,13},{5,3},... | collective-permute-start | bytes 1572872 | tf_op jit(solution)/shard_map/ppermute | solution.py:29
  11.5 0.0 collective-permute-done.other_ref
  11.5 0.0 copy-start
  11.5 1.6 %copy-done = bf16[1,64,128,128]{3,2,1,0:T(8,128)(2,1)S(1)} copy-done((bf16[1,64,128,128]{3,2,1,0:T(8,128)(2,1)S(1)}, bf16[1,64,128,128]{3,2,1,0:T(8,128)(2,1)}, u32[]{:S(2)}) %copy-start) | copy-done | bytes 2097176
  13.1 0.0 copy-start.2
  13.1 1.0 %copy-done.2 = bf16[512,512]{1,0:T(8,128)(2,1)S(1)} copy-done((bf16[512,512]{1,0:T(8,128)(2,1)S(1)}, bf16[512,512]{1,0:T(8,128)(2,1)}, u32[]{:S(2)}) %copy-start.2) | copy-done | bytes 524312
  14.1 0.0 copy-start.3
  14.1 1.0 %copy-done.3 = bf16[512,512]{1,0:T(8,128)(2,1)S(1)} copy-done((bf16[512,512]{1,0:T(8,128)(2,1)S(1)}, bf16[512,512]{1,0:T(8,128)(2,1)}, u32[]{:S(2)}) %copy-start.3) | copy-done | bytes 524312
  15.1 0.0 copy-start.6
  15.1 0.7 %copy-done.6 = f32[512]{0:T(512)S(1)} copy-done((f32[512]{0:T(512)S(1)}, f32[512]{0:T(512)}, u32[]{:S(2)}) %copy-start.6) | copy-done | bytes 2072
  15.8 0.0 copy-start.9
  15.8 0.7 copy-done.9
  16.5 0.0 copy-start.10
  16.5 0.7 copy-done.10
  17.1 0.0 copy-start.11
  17.1 1.0 %copy-done.11 = bf16[512,512]{1,0:T(8,128)(2,1)S(1)} copy-done((bf16[512,512]{1,0:T(8,128)(2,1)S(1)}, bf16[512,512]{1,0:T(8,128)(2,1)}, u32[]{:S(2)}) %copy-start.11) | copy-done | bytes 524312
  18.2 0.0 copy-start.12
  18.2 1.0 %copy-done.12 = bf16[512,512]{1,0:T(8,128)(2,1)S(1)} copy-done((bf16[512,512]{1,0:T(8,128)(2,1)S(1)}, bf16[512,512]{1,0:T(8,128)(2,1)}, u32[]{:S(2)}) %copy-start.12) | copy-done | bytes 524312
  19.2 0.0 copy-start.1
  19.2 4.6 %own_tiles.1 = (f32[4,128,512]{2,1,0:T(8,128)S(1)}, bf16[8,4,256,128]{3,2,1,0:T(8,128)(2,1)S(1)}, bf16[8,4,256,128]{3,2,1,0:T(8,128)(2,1)S(1)}) custom-call(s32[1,64]{1,0:T(1,128)S(1)} %copy-done.9, s32[1,64]{1,0:T(1,128)S(1)} %copy-done.10, s32[1,1]{1,0:T(1,128)S(6)} %copy.12.live_ref, bf16[512,512]{1,0:T(8,128)(2,1)S(1)} %copy-done.3, ...), custom_call_target="tpu_custom_call" | custom-call | flops 1986422400 | bytes 8388608 | tf_op jit(solution)/shard_map/own_tiles/pallas_call | solution.py:187
  23.9 0.0 collective-permute-done.1.refs_0_
  23.9 0.0 collective-permute-done.2.refs_1_
  23.9 0.0 collective-permute-done.3.refs_2_
  23.9 0.0 copy-done.1
  23.9 0.0 copy-start.7
  23.9 11.0 %near_tiles.1 = (bf16[512,512]{1,0:T(8,128)(2,1)S(1)}, bf16[512,512]{1,0:T(8,128)(2,1)S(1)}, bf16[512,512]{1,0:T(8,128)(2,1)S(1)}) custom-call(s32[1,64]{1,0:T(1,128)S(1)} %copy-done.9, s32[1,64]{1,0:T(1,128)S(1)} %copy-done.10, s32[1,1]{1,0:T(1,128)S(6)} %copy.12.live_ref, f32[1,512]{1,0:T(1,128)S(1)} %bitcast.7, bf16[512,512]{1,0:T(8,128)(2,1)S(1)} %copy-done.2, ...), custom_call_target="tpu_custom_call" | custom-call | flops 5959267328 | bytes 8388608 | tf_op jit(solution)/shard_map/near_tiles/pallas_call | solution.py:199
  34.9 2.1 %collective-permute-start.4 = (bf16[512,512]{1,0:T(8,128)(2,1)S(1)}, bf16[512,512]{1,0:T(8,128)(2,1)S(1)}, u32[]{:S(2)}, u32[]{:S(2)}) collective-permute-start(bf16[512,512]{1,0:T(8,128)(2,1)S(1)} %get-tuple-element.14), channel_id=1, source_target_pairs={{0,2},{4,6},{8,10},{12,14},{2,0},{6,4},{10,8},{14,12},{1,3},{5,7},... | collective-permute-start | bytes 1572872 | tf_op jit(solution)/shard_map/ppermute | solution.py:29
  37.0 5.4 %collective-permute-start.5 = (bf16[512,512]{1,0:T(8,128)(2,1)S(1)}, bf16[512,512]{1,0:T(8,128)(2,1)S(1)}, u32[]{:S(2)}, u32[]{:S(2)}) collective-permute-start(bf16[512,512]{1,0:T(8,128)(2,1)S(1)} %get-tuple-element.15), channel_id=1, source_target_pairs={{0,4},{2,6},{4,8},{6,10},{8,12},{10,14},{1,5},{3,7},{5,9},{7,11},{... | collective-permute-start | bytes 1572872 | tf_op jit(solution)/shard_map/ppermute | solution.py:23
  42.4 0.0 copy-start.4
  42.4 0.0 copy-start.5
  42.4 0.0 copy-start.8
  42.4 1.4 %collective-permute-start.6 = (bf16[512,512]{1,0:T(8,128)(2,1)S(1)}, bf16[512,512]{1,0:T(8,128)(2,1)S(1)}, u32[]{:S(2)}, u32[]{:S(2)}) collective-permute-start(bf16[512,512]{1,0:T(8,128)(2,1)S(1)} %get-tuple-element.16), channel_id=1, source_target_pairs={{4,0},{6,2},{8,4},{10,6},{12,8},{14,10},{5,1},{7,3},{9,5},{11,7},{... | collective-permute-start | bytes 1572872 | tf_op jit(solution)/shard_map/ppermute | solution.py:23
  43.8 0.0 collective-permute-done.7.refs_0_
  43.8 0.0 copy-done.7
  43.8 3.2 %diagonal_tiles.1 = bf16[512,512]{1,0:T(8,128)(2,1)S(1)} custom-call(s32[1,64]{1,0:T(1,128)S(1)} %copy-done.9, s32[1,64]{1,0:T(1,128)S(1)} %copy-done.10, s32[1,1]{1,0:T(1,128)S(6)} %copy.12.live_ref, f32[1,512]{1,0:T(1,128)S(1)} %bitcast.8, bf16[512,512]{1,0:T(8,128)(2,1)S(1)} %copy-done.2, bf16[64,128,128]{2,1,0:T(8,128)(2,1)S(1)} %bitcast.5, ...), custom_call_target="tpu_custom_call" | custom-call | flops 1986422400 | bytes 8388608 | tf_op jit(solution)/shard_map/diagonal_tiles/pallas_call | solution.py:199
  47.1 6.9 %collective-permute-start.8 = (bf16[512,512]{1,0:T(8,128)(2,1)S(1)}, bf16[512,512]{1,0:T(8,128)(2,1)S(1)}, u32[]{:S(2)}, u32[]{:S(2)}) collective-permute-start(bf16[512,512]{1,0:T(8,128)(2,1)S(1)} %diagonal_tiles.1), channel_id=1, source_target_pairs={{2,4},{6,8},{10,12},{4,2},{8,6},{12,10},{3,5},{7,9},{11,13},{5,3},... | collective-permute-start | bytes 1572872 | tf_op jit(solution)/shard_map/ppermute | solution.py:29
  54.0 0.0 collective-permute-done.4.a_ref
  54.1 0.0 collective-permute-done.5.b_ref
  54.1 0.7 collective-permute-done.6.c_ref
  54.7 11.5 %collective-permute-done.8.d_ref = bf16[512,512]{1,0:T(8,128)(2,1)S(1)} collective-permute-done((bf16[512,512]{1,0:T(8,128)(2,1)S(1)}, bf16[512,512]{1,0:T(8,128)(2,1)S(1)}, u32[]{:S(2)}, u32[]{:S(2)}) %collective-permute-start.8) | collective-permute-done | bytes 524320 | tf_op jit(solution)/shard_map/ppermute | solution.py:29
  66.3 0.0 copy-done.4
  66.3 0.0 copy-done.5
  66.3 0.0 copy-done.8
  66.3 1.6 %mix.1 = bf16[512,512]{1,0:T(8,128)(2,1)} custom-call(bf16[512,512]{1,0:T(8,128)(2,1)S(1)} %copy-done.4, f32[1,512]{1,0:T(1,128)S(1)} %bitcast.9, bf16[512,512]{1,0:T(8,128)(2,1)S(1)} %copy-done.5, f32[4,128,512]{2,1,0:T(8,128)S(1)} %get-tuple-element.11.own_ref, bf16[512,512]{1,0:T(8,128)(2,1)S(1)} %collective-permute-done.4.a_ref, ...), custom_call_target="tpu_custom_call" | custom-call | flops 268435456 | bytes 4194304 | tf_op jit(solution)/shard_map/mix/pallas_call | solution.py:217
Async XLA Ops:
  0.0 11.5 %collective-permute-start = (bf16[512,512]{1,0:T(8,128)(2,1)}, bf16[512,512]{1,0:T(8,128)(2,1)S(1)}, u32[]{:S(2)}, u32[]{:S(2)}) collective-permute-start(bf16[512,512]{1,0:T(8,128)(2,1)} %nodes_ref.3), channel_id=1, source_target_pairs={{0,1},{1,0},{2,3},{3,2},{4,5},{5,4},{6,7},{7,6},{8,9},{9,8},{10,11... | collective-permute-start | bytes 1572872 | tf_op jit(solution)/shard_map/ppermute | solution.py:181
  0.0 23.9 %collective-permute-start.1 = (bf16[512,512]{1,0:T(8,128)(2,1)}, bf16[512,512]{1,0:T(8,128)(2,1)S(1)}, u32[]{:S(2)}, u32[]{:S(2)}) collective-permute-start(bf16[512,512]{1,0:T(8,128)(2,1)} %nodes_ref.3), channel_id=1, source_target_pairs={{0,2},{4,6},{8,10},{12,14},{2,0},{6,4},{10,8},{14,12},{1,3},{5,7},... | collective-permute-start | bytes 1572872 | tf_op jit(solution)/shard_map/ppermute | solution.py:29
  0.5 23.3 %collective-permute-start.2 = (bf16[512,512]{1,0:T(8,128)(2,1)}, bf16[512,512]{1,0:T(8,128)(2,1)S(1)}, u32[]{:S(2)}, u32[]{:S(2)}) collective-permute-start(bf16[512,512]{1,0:T(8,128)(2,1)} %nodes_ref.3), channel_id=1, source_target_pairs={{4,0},{6,2},{8,4},{10,6},{12,8},{14,10},{5,1},{7,3},{9,5},{11,7},{... | collective-permute-start | bytes 1572872 | tf_op jit(solution)/shard_map/ppermute | solution.py:23
  1.8 22.0 %collective-permute-start.3 = (bf16[512,512]{1,0:T(8,128)(2,1)}, bf16[512,512]{1,0:T(8,128)(2,1)S(1)}, u32[]{:S(2)}, u32[]{:S(2)}) collective-permute-start(bf16[512,512]{1,0:T(8,128)(2,1)} %nodes_ref.3), channel_id=1, source_target_pairs={{0,4},{2,6},{4,8},{6,10},{8,12},{10,14},{1,5},{3,7},{5,9},{7,11},{... | collective-permute-start | bytes 1572872 | tf_op jit(solution)/shard_map/ppermute | solution.py:23
  6.4 37.4 %collective-permute-start.7 = (bf16[512,512]{1,0:T(8,128)(2,1)}, bf16[512,512]{1,0:T(8,128)(2,1)S(1)}, u32[]{:S(2)}, u32[]{:S(2)}) collective-permute-start(bf16[512,512]{1,0:T(8,128)(2,1)} %nodes_ref.3), channel_id=1, source_target_pairs={{2,4},{6,8},{10,12},{4,2},{8,6},{12,10},{3,5},{7,9},{11,13},{5,3},... | collective-permute-start | bytes 1572872 | tf_op jit(solution)/shard_map/ppermute | solution.py:29
  11.5 1.6 %copy-start = (bf16[1,64,128,128]{3,2,1,0:T(8,128)(2,1)S(1)}, bf16[1,64,128,128]{3,2,1,0:T(8,128)(2,1)}, u32[]{:S(2)}) copy-start(bf16[1,64,128,128]{3,2,1,0:T(8,128)(2,1)} %param.18) | copy-start | bytes 6291460
  13.1 1.0 %copy-start.2 = (bf16[512,512]{1,0:T(8,128)(2,1)S(1)}, bf16[512,512]{1,0:T(8,128)(2,1)}, u32[]{:S(2)}) copy-start(bf16[512,512]{1,0:T(8,128)(2,1)} %wq_ref.5) | copy-start | bytes 1572868
  14.1 1.0 %copy-start.3 = (bf16[512,512]{1,0:T(8,128)(2,1)S(1)}, bf16[512,512]{1,0:T(8,128)(2,1)}, u32[]{:S(2)}) copy-start(bf16[512,512]{1,0:T(8,128)(2,1)} %nodes_ref.3) | copy-start | bytes 1572868
  15.1 0.7 %copy-start.6 = (f32[512]{0:T(512)S(1)}, f32[512]{0:T(512)}, u32[]{:S(2)}) copy-start(f32[512]{0:T(512)} %param.12) | copy-start | bytes 6148
  15.8 0.7 copy-start.9
  16.5 0.7 copy-start.10
  17.1 1.0 %copy-start.11 = (bf16[512,512]{1,0:T(8,128)(2,1)S(1)}, bf16[512,512]{1,0:T(8,128)(2,1)}, u32[]{:S(2)}) copy-start(bf16[512,512]{1,0:T(8,128)(2,1)} %wk_ref.1) | copy-start | bytes 1572868
  18.2 1.0 %copy-start.12 = (bf16[512,512]{1,0:T(8,128)(2,1)S(1)}, bf16[512,512]{1,0:T(8,128)(2,1)}, u32[]{:S(2)}) copy-start(bf16[512,512]{1,0:T(8,128)(2,1)} %wv_ref.1) | copy-start | bytes 1572868
  19.2 4.7 %copy-start.1 = (bf16[1,64,128,128]{3,2,1,0:T(8,128)(2,1)S(1)}, bf16[1,64,128,128]{3,2,1,0:T(8,128)(2,1)}, u32[]{:S(2)}) copy-start(bf16[1,64,128,128]{3,2,1,0:T(8,128)(2,1)} %param.18) | copy-start | bytes 6291460
  23.9 19.9 %copy-start.7 = (f32[512]{0:T(512)S(1)}, f32[512]{0:T(512)}, u32[]{:S(2)}) copy-start(f32[512]{0:T(512)} %param.12) | copy-start | bytes 6148
  34.9 19.1 %collective-permute-start.4 = (bf16[512,512]{1,0:T(8,128)(2,1)S(1)}, bf16[512,512]{1,0:T(8,128)(2,1)S(1)}, u32[]{:S(2)}, u32[]{:S(2)}) collective-permute-start(bf16[512,512]{1,0:T(8,128)(2,1)S(1)} %get-tuple-element.14), channel_id=1, source_target_pairs={{0,2},{4,6},{8,10},{12,14},{2,0},{6,4},{10,8},{14,12},{1,3},{5,7},... | collective-permute-start | bytes 1572872 | tf_op jit(solution)/shard_map/ppermute | solution.py:29
  37.0 17.1 %collective-permute-start.5 = (bf16[512,512]{1,0:T(8,128)(2,1)S(1)}, bf16[512,512]{1,0:T(8,128)(2,1)S(1)}, u32[]{:S(2)}, u32[]{:S(2)}) collective-permute-start(bf16[512,512]{1,0:T(8,128)(2,1)S(1)} %get-tuple-element.15), channel_id=1, source_target_pairs={{0,4},{2,6},{4,8},{6,10},{8,12},{10,14},{1,5},{3,7},{5,9},{7,11},{... | collective-permute-start | bytes 1572872 | tf_op jit(solution)/shard_map/ppermute | solution.py:23
  42.4 23.9 %copy-start.4 = (bf16[512,512]{1,0:T(8,128)(2,1)S(1)}, bf16[512,512]{1,0:T(8,128)(2,1)}, u32[]{:S(2)}) copy-start(bf16[512,512]{1,0:T(8,128)(2,1)} %nodes_ref.3) | copy-start | bytes 1572868
  42.4 23.9 %copy-start.5 = (bf16[512,512]{1,0:T(8,128)(2,1)S(1)}, bf16[512,512]{1,0:T(8,128)(2,1)}, u32[]{:S(2)}) copy-start(bf16[512,512]{1,0:T(8,128)(2,1)} %w_out_ref.1) | copy-start | bytes 1572868
  42.4 23.9 %copy-start.8 = (f32[512]{0:T(512)S(1)}, f32[512]{0:T(512)}, u32[]{:S(2)}) copy-start(f32[512]{0:T(512)} %param.17) | copy-start | bytes 6148
  42.4 12.3 %collective-permute-start.6 = (bf16[512,512]{1,0:T(8,128)(2,1)S(1)}, bf16[512,512]{1,0:T(8,128)(2,1)S(1)}, u32[]{:S(2)}, u32[]{:S(2)}) collective-permute-start(bf16[512,512]{1,0:T(8,128)(2,1)S(1)} %get-tuple-element.16), channel_id=1, source_target_pairs={{4,0},{6,2},{8,4},{10,6},{12,8},{14,10},{5,1},{7,3},{9,5},{11,7},{... | collective-permute-start | bytes 1572872 | tf_op jit(solution)/shard_map/ppermute | solution.py:23
  47.1 19.2 %collective-permute-start.8 = (bf16[512,512]{1,0:T(8,128)(2,1)S(1)}, bf16[512,512]{1,0:T(8,128)(2,1)S(1)}, u32[]{:S(2)}, u32[]{:S(2)}) collective-permute-start(bf16[512,512]{1,0:T(8,128)(2,1)S(1)} %diagonal_tiles.1), channel_id=1, source_target_pairs={{2,4},{6,8},{10,12},{4,2},{8,6},{12,10},{3,5},{7,9},{11,13},{5,3},... | collective-permute-start | bytes 1572872 | tf_op jit(solution)/shard_map/ppermute | solution.py:29

commit v2 on v1

v2 whole, which is shorter than its diff:
```python
import functools

import jax
import jax.numpy as jnp
from jax import lax
from jax.experimental import pallas as pl
from jax.experimental.pallas import tpu as pltpu
from jax.sharding import PartitionSpec as P

HEADS = 8
HALO = 2
UNROLL = 4
EPSILON = 1e-05
BF16 = jnp.bfloat16
F32 = jnp.float32
VMEM = pl.BlockSpec(memory_space=pltpu.VMEM)
SMEM = pl.BlockSpec(memory_space=pltpu.SMEM)
ANY = pl.BlockSpec(memory_space=pl.ANY)
HBM = pl.BlockSpec(memory_space=pltpu.HBM)


def swap(block, axis, stride, parity):
    count = lax.axis_size(axis)
    pairs = [(i, i + stride) for i in range(count - stride) if i // stride % 2 == parity]
    return lax.ppermute(block, axis, pairs + [(j, i) for i, j in pairs])


def partner_offset(axis, stride, parity):
    return jnp.where(lax.axis_index(axis) // stride % 2 == parity, stride, -stride)


def rms_scale(features, gain):
    features = features.astype(F32)
    scale = lax.rsqrt(jnp.mean(features * features, axis=-1, keepdims=True) + EPSILON)
    return features * scale * gain


def project(normed, weight_ref):
    return jnp.dot(normed, weight_ref[...], preferred_element_type=F32).astype(BF16)


def scaled_query(normed, weight_ref):
    return project(normed, weight_ref) * BF16(1.0 / 16.0)


def split_heads(block):
    lane = lax.broadcasted_iota(jnp.int32, block.shape, 1)
    first = lane < block.shape[1] // 2
    zero = jnp.zeros_like(block)
    return jnp.concatenate([jnp.where(first, block, zero), jnp.where(first, zero, block)], axis=0)


def pack_heads(full, packed_ref, base):
    rows = packed_ref.shape[2] // 2
    wide = packed_ref.shape[3]
    for block in range(full.shape[0] // rows):
        for pair in range(packed_ref.shape[1]):
            packed_ref[base + block, pair] = split_heads(
                full[block * rows : (block + 1) * rows, pair * wide : (pair + 1) * wide]
            )


def visit_tiles(code, list_ref, weight_ref, query_ref, key_ref, value_ref, acc_ref):
    rows = weight_ref.shape[1]
    pairs = key_ref.shape[1]
    wide = key_ref.shape[3]
    acc_ref[...] = jnp.zeros_like(acc_ref)
    found = list_ref[code, 0]

    def step(index, carry):
        tiles, gates = [], []
        for u in range(UNROLL):
            place = index * UNROLL + u
            entry = list_ref[code, 1 + place]
            tile, source, target = entry & 1023, (entry >> 10) & 1023, entry >> 20
            half = jnp.where(place < found, 0.5, 0.0)
            weight = (weight_ref[tile].astype(F32) * half).astype(BF16)
            weight = jnp.concatenate([weight, weight], axis=1)
            target = pl.ds(pl.multiple_of(target * rows, rows), rows)
            tiles.append((source, target))
            gate = []
            for pair in range(pairs):
                scores = lax.dot_general(
                    query_ref[target, pair * wide : (pair + 1) * wide],
                    key_ref[source, pair],
                    (((1,), (1,)), ((), ())),
                    preferred_element_type=F32,
                )
                gate.append(jnp.tanh(scores.astype(BF16)) * weight + weight)
            gates.append(gate)
        sums = [
            [jnp.dot(gate[pair], value_ref[source, pair], preferred_element_type=F32) for pair in range(pairs)]
            for (source, _), gate in zip(tiles, gates)
        ]
        for (_, target), total in zip(tiles, sums):
            for pair in range(pairs):
                acc_ref[target, pair * wide : (pair + 1) * wide] += total[pair]
        return carry

    lax.fori_loop(0, pl.cdiv(found, UNROLL), step, 0)


def start_copies(pairs, sems):
    copies = [pltpu.make_async_copy(a, b, sems.at[i]) for i, (a, b) in enumerate(pairs)]
    for copy in copies:
        copy.start()
    return copies


def prepare_kernel(
    blocks, src_hbm, dst_hbm, nodes_hbm, gain_hbm, wk_hbm, wv_hbm, wq_hbm, weight_hbm, live_ref, other_ref,
    key_ref, value_ref, weight_ref, nodes_ref, gain_ref, wq_ref, list_out,
    wk_ref, wv_ref, src_ref, dst_ref, list_ref, sems,
):
    copies = start_copies(
        [
            (src_hbm, src_ref), (dst_hbm, dst_ref), (nodes_hbm, nodes_ref), (gain_hbm, gain_ref), (wk_hbm, wk_ref),
            (wv_hbm, wv_ref), (wq_hbm, wq_ref), (weight_hbm, weight_ref),
        ],
        sems,
    )
    for copy in copies[:2]:
        copy.wait()
    codes = list_ref.shape[0]
    for code in range(codes):
        list_ref[code, 0] = 0

    def collect(tile, carry):
        target = dst_ref[0, tile]
        code = target // blocks
        found = list_ref[code, 0] + 1
        list_ref[code, found] = tile + src_ref[0, tile] * 1024 + (target - code * blocks) * (1024 * 1024)
        list_ref[code, 0] = found
        return carry

    lax.fori_loop(0, live_ref[0, 0], collect, 0)
    for code in range(codes):
        found = list_ref[code, 0]
        for extra in range(UNROLL):
            list_ref[code, found + 1 + extra] = 0
    list_copy = pltpu.make_async_copy(list_ref, list_out, sems.at[len(copies)])
    list_copy.start()

    me = lax.axis_index("col")
    copies[3].wait()
    other = rms_scale(other_ref[...], gain_ref[...]).astype(BF16)
    copies[2].wait()
    normed = rms_scale(nodes_ref[...], gain_ref[...]).astype(BF16)
    copies[4].wait()
    pack_heads(project(normed, wk_ref), key_ref, me * blocks)
    pack_heads(project(other, wk_ref), key_ref, (1 - me) * blocks)
    copies[5].wait()
    pack_heads(project(normed, wv_ref), value_ref, me * blocks)
    pack_heads(project(other, wv_ref), value_ref, (1 - me) * blocks)
    copies[6].wait()
    copies[7].wait()
    list_copy.wait()


def tiles_kernel(place, list_hbm, gain_ref, wq_ref, weight_ref, key_ref, value_ref, nodes_ref, _, out_ref, *scratch):
    query_ref, list_ref, sem = scratch[:3]
    copy = pltpu.make_async_copy(list_hbm, list_ref, sem)
    copy.start()
    normed = rms_scale(nodes_ref[...], gain_ref[...]).astype(BF16)
    query_ref[...] = scaled_query(normed, wq_ref)
    copy.wait()
    code = HALO + (partner_offset("row", *place) if place else 0)
    sums = out_ref if out_ref.dtype == F32 else scratch[3]
    visit_tiles(code, list_ref, weight_ref, query_ref, key_ref, value_ref, sums)
    if out_ref.dtype != F32:
        out_ref[...] = sums[...].astype(BF16)


def add_kernel(sum_ref, part_ref, out_ref):
    out_ref[...] = sum_ref[...] + part_ref[...].astype(F32)


def last_kernel(nodes_ref, gain_ref, w_out_ref, sum_ref, part_ref, out_ref):
    aggregate = sum_ref[...] + part_ref[...].astype(F32)
    mixed = rms_scale(aggregate, gain_ref[...]).astype(BF16)
    update = jnp.dot(mixed, w_out_ref[...], preferred_element_type=F32)
    out_ref[...] = (nodes_ref[...].astype(F32) + update).astype(BF16)


def local(nodes, ln_gain, w_query, w_key, w_value, w_out, agg_gain, tile_weight, tile_src, tile_dst, tile_live):
    rows_dev, features = nodes.shape
    tile_count, tile_rows = tile_weight.shape[1], tile_weight.shape[-1]
    blocks = rows_dev // tile_rows
    pairs = HEADS // 2
    wide = features // pairs
    sources = lax.axis_size("col") * blocks
    weight = tile_weight[0]
    codes = 2 * HALO + 1
    params = pltpu.CompilerParams(vmem_limit_bytes=32 << 20)

    cost = pl.CostEstimate(flops=1 << 20, bytes_accessed=1 << 16, transcendentals=0)
    shape = jax.ShapeDtypeStruct
    block_bf16 = shape((rows_dev, features), BF16)
    block_f32 = shape((rows_dev, features), F32)
    packed = shape((sources, pairs, 2 * tile_rows, wide), BF16)
    lists = (codes, 1 + tile_count + UNROLL)
    square = pltpu.VMEM((features, features), BF16)

    def in_hbm(*arrays):
        return [pltpu.with_memory_space_constraint(array, pltpu.HBM) for array in arrays]

    places = ((1, 0), (2, 0), (2, 1), (1, 1))
    other = lax.ppermute(nodes, "col", [(0, 1), (1, 0)])
    arrived = {place: swap(nodes, "row", *place) for place in places[:3]}

    keys, values, weight_held, nodes_held, gain, wq, lists_out = pl.pallas_call(
        functools.partial(prepare_kernel, blocks),
        out_shape=(
            packed, packed, shape(weight.shape, BF16), block_bf16, shape((1, features), F32),
            shape(w_query.shape, BF16), shape(lists, jnp.int32),
        ),
        in_specs=[HBM] * 8 + [SMEM, VMEM],
        out_specs=(VMEM,) * 6 + (HBM,),
        scratch_shapes=[
            square, square, pltpu.SMEM(tile_src.shape, jnp.int32), pltpu.SMEM(tile_dst.shape, jnp.int32),
            pltpu.SMEM(lists, jnp.int32), pltpu.SemaphoreType.DMA((9,)),
        ],
        compiler_params=params,
        cost_estimate=cost,
        name="prepare",
    )(
        *in_hbm(tile_src, tile_dst, nodes, ln_gain.reshape(1, features), w_key, w_value, w_query, weight),
        tile_live,
        other,
    )
    arrived[places[3]] = swap(nodes_held, "row", *places[3])

    def tiles(name, place, block, after, out):
        return pl.pallas_call(
            functools.partial(tiles_kernel, place),
            out_shape=out,
            in_specs=[HBM] + [VMEM] * 6 + [ANY],
            out_specs=VMEM,
            scratch_shapes=[
                pltpu.VMEM((rows_dev, features), BF16), pltpu.SMEM(lists, jnp.int32), pltpu.SemaphoreType.DMA,
            ] + [pltpu.VMEM((rows_dev, features), F32)] * (out.dtype != F32),
            compiler_params=params,
            cost_estimate=cost,
            name=name,
        )(lists_out, gain, wq, weight_held, keys, values, block, after)

    last, returned = gain, []
    for place in places:
        last = tiles("tiles_%d_%d" % place, place, arrived[place], last, block_bf16)
        returned.append(swap(last, "row", *place))
    total = tiles("own_tiles", None, nodes_held, last, block_f32)
    for part in returned[:-1]:
        total = pl.pallas_call(
            add_kernel,
            out_shape=block_f32,
            in_specs=[VMEM] * 2,
            out_specs=VMEM,
            input_output_aliases={0: 0},
            compiler_params=params,
            cost_estimate=pl.CostEstimate(flops=1 << 18, bytes_accessed=2 << 20, transcendentals=0),
            name="add",
        )(total, part)

    return pl.pallas_call(
        last_kernel,
        out_shape=block_bf16,
        in_specs=[VMEM] * 5,
        out_specs=VMEM,
        compiler_params=params,
        cost_estimate=cost,
        name="mix",
    )(nodes, agg_gain.reshape(1, features), w_out, total, returned[-1])


def solution(mesh):
    return jax.shard_map(
        local,
        mesh=mesh,
        in_specs=(
            P(("slide", "row", "col"), None),
            P(),
            P(),
            P(),
            P(),
            P(),
            P(),
            P(("slide", "row"), "col", None, None),
            P(("slide", "row"), "col"),
            P(("slide", "row"), "col"),
            P(("slide", "row"), "col"),
        ),
        out_specs=P(("slide", "row", "col"), None),
        check_vma=False,
    )
```

time: 68.7 us -> 55.5 us (0.81)
  the two profiles are of different devices: /device:TPU:6 before, /device:TPU:21 now
where the time goes in v2:
time: 55.5 us; the launch traced here: 55.8 us
  starting transfers between devices  21.1 us (38%)
  waiting for transfers between devices  21 us (38%)
  Pallas kernels  13 us (23%)
  between operations  0.8 us (1%)
    ppermute x8, waiting for transfers between devices, swap(): return lax.ppermute(block, axis, pairs + [(j, i) for i, j in pairs])  21 us
    ppermute x8, starting transfers between devices, swap(): return lax.ppermute(block, axis, pairs + [(j, i) for i, j in pairs])  20.4 us
    pallas_call x5, Pallas kernels, tiles(): pl.pallas_call(functools.partial(tiles_kernel, place), out_shape=out, in_...  7.96 us
    pallas_call x1, Pallas kernels, local(): pl.pallas_call(functools.partial(prepare_kernel, blocks), out_shape=(pack...  3.03 us
    pallas_call x1, Pallas kernels, local(): pl.pallas_call(last_kernel, out_shape=block_bf16, in_specs=[VMEM] * 5, ou...  1.36 us
  transfers between devices with their start and end apart: 9, of which 4 were waited for; matrix products, arithmetic and copies ran while one was open for 0% of the time, Pallas kernels for 21%

profile of v2, /device:TPU:21, one launch (start us, length us, event | category | flops | bytes accessed | tf_op | source)
XLA Modules:
  0.0 55.8 jit_solution(9071120892694661431)
XLA Ops:
  0.0 0.7 %collective-permute-start = (bf16[512,512]{1,0:T(8,128)(2,1)}, bf16[512,512]{1,0:T(8,128)(2,1)S(1)}, u32[]{:S(2)}, u32[]{:S(2)}) collective-permute-start(bf16[512,512]{1,0:T(8,128)(2,1)} %nodes_ref.1), channel_id=1, source_target_pairs={{0,1},{1,0},{2,3},{3,2},{4,5},{5,4},{6,7},{7,6},{8,9},{9,8},{10,11... | collective-permute-start | bytes 1572872 | tf_op jit(solution)/shard_map/ppermute | solution.py:208
  0.7 1.2 %collective-permute-start.4 = (bf16[512,512]{1,0:T(8,128)(2,1)}, bf16[512,512]{1,0:T(8,128)(2,1)S(1)}, u32[]{:S(2)}, u32[]{:S(2)}) collective-permute-start(bf16[512,512]{1,0:T(8,128)(2,1)} %nodes_ref.1), channel_id=1, source_target_pairs={{0,2},{4,6},{8,10},{12,14},{2,0},{6,4},{10,8},{14,12},{1,3},{5,7},... | collective-permute-start | bytes 1572872 | tf_op jit(solution)/shard_map/ppermute | solution.py:25
  1.9 1.3 %collective-permute-start.3 = (bf16[512,512]{1,0:T(8,128)(2,1)}, bf16[512,512]{1,0:T(8,128)(2,1)S(1)}, u32[]{:S(2)}, u32[]{:S(2)}) collective-permute-start(bf16[512,512]{1,0:T(8,128)(2,1)} %nodes_ref.1), channel_id=1, source_target_pairs={{0,4},{2,6},{8,12},{10,14},{4,0},{6,2},{12,8},{14,10},{1,5},{3,7},... | collective-permute-start | bytes 1572872 | tf_op jit(solution)/shard_map/ppermute | solution.py:25
  3.2 1.9 %collective-permute-start.2 = (bf16[512,512]{1,0:T(8,128)(2,1)}, bf16[512,512]{1,0:T(8,128)(2,1)S(1)}, u32[]{:S(2)}, u32[]{:S(2)}) collective-permute-start(bf16[512,512]{1,0:T(8,128)(2,1)} %nodes_ref.1), channel_id=1, source_target_pairs={{4,8},{6,10},{8,4},{10,6},{5,9},{7,11},{9,5},{11,7},{20,24},{22,26... | collective-permute-start | bytes 1572872 | tf_op jit(solution)/shard_map/ppermute | solution.py:25
  5.7 0.0 collective-permute-done.other_ref
  5.8 3.0 %prepare.1 = (bf16[8,4,256,128]{3,2,1,0:T(8,128)(2,1)S(1)}, bf16[8,4,256,128]{3,2,1,0:T(8,128)(2,1)S(1)}, bf16[64,128,128]{2,1,0:T(8,128)(2,1)S(1)}, bf16[512,51...) custom-call(s32[1,64]{1,0:T(1,128)} %src_hbm.1, ...), custom_call_target="tpu_custom_call" | custom-call | flops 1048576 | bytes 65536 | tf_op jit(solution)/shard_map/prepare/pallas_call | solution.py:211
  8.8 3.5 %collective-permute-start.1 = (bf16[512,512]{1,0:T(8,128)(2,1)S(1)}, bf16[512,512]{1,0:T(8,128)(2,1)S(1)}, u32[]{:S(2)}, u32[]{:S(2)}) collective-permute-start(bf16[512,512]{1,0:T(8,128)(2,1)S(1)} %get-tuple-element.18.nodes_ref), channel_id=1, source_target_pairs={{2,4},{6,8},{10,12},{4,2},{8,6},{12,10},{3,5},{7,9},{11,13},{5,3},... | collective-permute-start | bytes 1572872 | tf_op jit(solution)/shard_map/ppermute | solution.py:25
  12.3 2.2 %collective-permute-done.4.nodes_ref = bf16[512,512]{1,0:T(8,128)(2,1)S(1)} collective-permute-done((bf16[512,512]{1,0:T(8,128)(2,1)}, bf16[512,512]{1,0:T(8,128)(2,1)S(1)}, u32[]{:S(2)}, u32[]{:S(2)}) %collective-permute-start.4) | collective-permute-done | bytes 524320 | tf_op jit(solution)/shard_map/ppermute | solution.py:25
  14.4 2.2 %tiles_1_0.1._ = bf16[512,512]{1,0:T(8,128)(2,1)S(1)} custom-call(s32[5,69]{1,0:T(8,128)S(1)} %get-tuple-element.12.list_hbm, f32[1,512]{1,0:T(1,128)S(1)} %get-tuple-element.13.gain_ref._, bf16[512,512]{1,0:T(8,128)(2,1)S(1)} %get-tuple-element.14.wq_ref, bf16[64,128,128]{2,1,0:T(8,128)(2,1)S(1)} %get-tuple-element.15.weight_ref, ...), custom_call_target="tpu_custom_call" | custom-call | flops 1048576 | bytes 65536 | tf_op jit(solution)/shard_map/tiles_1_0/pallas_call | solution.py:234
  16.6 2.0 %collective-permute-start.5 = (bf16[512,512]{1,0:T(8,128)(2,1)S(1)}, bf16[512,512]{1,0:T(8,128)(2,1)S(1)}, u32[]{:S(2)}, u32[]{:S(2)}) collective-permute-start(bf16[512,512]{1,0:T(8,128)(2,1)S(1)} %tiles_1_0.1._), channel_id=1, source_target_pairs={{0,2},{4,6},{8,10},{12,14},{2,0},{6,4},{10,8},{14,12},{1,3},{5,7},... | collective-permute-start | bytes 1572872 | tf_op jit(solution)/shard_map/ppermute | solution.py:25
  18.7 0.0 collective-permute-done.3.nodes_ref
  18.7 1.4 %tiles_2_0.1._ = bf16[512,512]{1,0:T(8,128)(2,1)S(1)} custom-call(s32[5,69]{1,0:T(8,128)S(1)} %get-tuple-element.12.list_hbm, f32[1,512]{1,0:T(1,128)S(1)} %get-tuple-element.13.gain_ref._, bf16[512,512]{1,0:T(8,128)(2,1)S(1)} %get-tuple-element.14.wq_ref, bf16[64,128,128]{2,1,0:T(8,128)(2,1)S(1)} %get-tuple-element.15.weight_ref, ...), custom_call_target="tpu_custom_call" | custom-call | flops 1048576 | bytes 65536 | tf_op jit(solution)/shard_map/tiles_2_0/pallas_call | solution.py:234
  20.1 3.9 %collective-permute-start.6 = (bf16[512,512]{1,0:T(8,128)(2,1)S(1)}, bf16[512,512]{1,0:T(8,128)(2,1)S(1)}, u32[]{:S(2)}, u32[]{:S(2)}) collective-permute-start(bf16[512,512]{1,0:T(8,128)(2,1)S(1)} %tiles_2_0.1._), channel_id=1, source_target_pairs={{0,4},{2,6},{8,12},{10,14},{4,0},{6,2},{12,8},{14,10},{1,5},{3,7},... | collective-permute-start | bytes 1572872 | tf_op jit(solution)/shard_map/ppermute | solution.py:25
  24.0 0.0 collective-permute-done.2.nodes_ref
  24.0 1.5 %tiles_2_1.1._ = bf16[512,512]{1,0:T(8,128)(2,1)S(1)} custom-call(s32[5,69]{1,0:T(8,128)S(1)} %get-tuple-element.12.list_hbm, f32[1,512]{1,0:T(1,128)S(1)} %get-tuple-element.13.gain_ref._, bf16[512,512]{1,0:T(8,128)(2,1)S(1)} %get-tuple-element.14.wq_ref, bf16[64,128,128]{2,1,0:T(8,128)(2,1)S(1)} %get-tuple-element.15.weight_ref, ...), custom_call_target="tpu_custom_call" | custom-call | flops 1048576 | bytes 65536 | tf_op jit(solution)/shard_map/tiles_2_1/pallas_call | solution.py:234
  25.5 1.9 %collective-permute-start.7 = (bf16[512,512]{1,0:T(8,128)(2,1)S(1)}, bf16[512,512]{1,0:T(8,128)(2,1)S(1)}, u32[]{:S(2)}, u32[]{:S(2)}) collective-permute-start(bf16[512,512]{1,0:T(8,128)(2,1)S(1)} %tiles_2_1.1._), channel_id=1, source_target_pairs={{4,8},{6,10},{8,4},{10,6},{5,9},{7,11},{9,5},{11,7},{20,24},{22,26... | collective-permute-start | bytes 1572872 | tf_op jit(solution)/shard_map/ppermute | solution.py:25
  27.4 2.1 %collective-permute-done.1.nodes_ref = bf16[512,512]{1,0:T(8,128)(2,1)S(1)} collective-permute-done((bf16[512,512]{1,0:T(8,128)(2,1)S(1)}, bf16[512,512]{1,0:T(8,128)(2,1)S(1)}, u32[]{:S(2)}, u32[]{:S(2)}) %collective-permute-start.1) | collective-permute-done | bytes 524320 | tf_op jit(solution)/shard_map/ppermute | solution.py:25
  29.4 1.4 %tiles_1_1.1._ = bf16[512,512]{1,0:T(8,128)(2,1)S(1)} custom-call(s32[5,69]{1,0:T(8,128)S(1)} %get-tuple-element.12.list_hbm, f32[1,512]{1,0:T(1,128)S(1)} %get-tuple-element.13.gain_ref._, bf16[512,512]{1,0:T(8,128)(2,1)S(1)} %get-tuple-element.14.wq_ref, bf16[64,128,128]{2,1,0:T(8,128)(2,1)S(1)} %get-tuple-element.15.weight_ref, ...), custom_call_target="tpu_custom_call" | custom-call | flops 1048576 | bytes 65536 | tf_op jit(solution)/shard_map/tiles_1_1/pallas_call | solution.py:234
  30.9 4.7 %collective-permute-start.8 = (bf16[512,512]{1,0:T(8,128)(2,1)S(1)}, bf16[512,512]{1,0:T(8,128)(2,1)S(1)}, u32[]{:S(2)}, u32[]{:S(2)}) collective-permute-start(bf16[512,512]{1,0:T(8,128)(2,1)S(1)} %tiles_1_1.1._), channel_id=1, source_target_pairs={{2,4},{6,8},{10,12},{4,2},{8,6},{12,10},{3,5},{7,9},{11,13},{5,3},... | collective-permute-start | bytes 1572872 | tf_op jit(solution)/shard_map/ppermute | solution.py:25
  35.6 1.4 %own_tiles.1.sum_ref = f32[512,512]{1,0:T(8,128)S(1)} custom-call(s32[5,69]{1,0:T(8,128)S(1)} %get-tuple-element.12.list_hbm, f32[1,512]{1,0:T(1,128)S(1)} %get-tuple-element.13.gain_ref._, bf16[512,512]{1,0:T(8,128)(2,1)S(1)} %get-tuple-element.14.wq_ref, bf16[64,128,128]{2,1,0:T(8,128)(2,1)S(1)} %get-tuple-element.15.weight_ref, ...), custom_call_target="tpu_custom_call" | custom-call | flops 1048576 | bytes 65536 | tf_op jit(solution)/shard_map/own_tiles/pallas_call | solution.py:234
  37.0 4.2 %collective-permute-done.5.part_ref = bf16[512,512]{1,0:T(8,128)(2,1)S(1)} collective-permute-done((bf16[512,512]{1,0:T(8,128)(2,1)S(1)}, bf16[512,512]{1,0:T(8,128)(2,1)S(1)}, u32[]{:S(2)}, u32[]{:S(2)}) %collective-permute-start.5) | collective-permute-done | bytes 524320 | tf_op jit(solution)/shard_map/ppermute | solution.py:25
  41.3 0.2 add.3.sum_ref
  41.5 0.0 copy-start
  41.5 0.0 copy-start.1
  41.5 0.0 copy-start.2
  41.5 0.0 collective-permute-done.6.part_ref
  41.5 0.2 add.4.sum_ref
  41.7 0.0 collective-permute-done.7.part_ref
  41.7 0.2 add.5.sum_ref
  41.9 12.5 %collective-permute-done.8.part_ref = bf16[512,512]{1,0:T(8,128)(2,1)S(1)} collective-permute-done((bf16[512,512]{1,0:T(8,128)(2,1)S(1)}, bf16[512,512]{1,0:T(8,128)(2,1)S(1)}, u32[]{:S(2)}, u32[]{:S(2)}) %collective-permute-start.8) | collective-permute-done | bytes 524320 | tf_op jit(solution)/shard_map/ppermute | solution.py:25
  54.5 0.0 copy-done
  54.5 0.0 copy-done.1
  54.5 0.0 copy-done.2
  54.5 1.4 %mix.1 = bf16[512,512]{1,0:T(8,128)(2,1)} custom-call(bf16[512,512]{1,0:T(8,128)(2,1)S(1)} %copy-done, f32[1,512]{1,0:T(1,128)S(1)} %bitcast.3, bf16[512,512]{1,0:T(8,128)(2,1)S(1)} %copy-done.1, f32[512,512]{1,0:T(8,128)S(1)} %add.5.sum_ref, bf16[512,512]{1,0:T(8,128)(2,1)S(1)} %collective-permute-done.8.part_ref), custom_call_target="tpu_custom_call" | custom-call | flops 1048576 | bytes 65536 | tf_op jit(solution)/shard_map/mix/pallas_call | solution.py:264
Async XLA Ops:
  0.0 5.8 %collective-permute-start = (bf16[512,512]{1,0:T(8,128)(2,1)}, bf16[512,512]{1,0:T(8,128)(2,1)S(1)}, u32[]{:S(2)}, u32[]{:S(2)}) collective-permute-start(bf16[512,512]{1,0:T(8,128)(2,1)} %nodes_ref.1), channel_id=1, source_target_pairs={{0,1},{1,0},{2,3},{3,2},{4,5},{5,4},{6,7},{7,6},{8,9},{9,8},{10,11... | collective-permute-start | bytes 1572872 | tf_op jit(solution)/shard_map/ppermute | solution.py:208
  0.7 13.8 %collective-permute-start.4 = (bf16[512,512]{1,0:T(8,128)(2,1)}, bf16[512,512]{1,0:T(8,128)(2,1)S(1)}, u32[]{:S(2)}, u32[]{:S(2)}) collective-permute-start(bf16[512,512]{1,0:T(8,128)(2,1)} %nodes_ref.1), channel_id=1, source_target_pairs={{0,2},{4,6},{8,10},{12,14},{2,0},{6,4},{10,8},{14,12},{1,3},{5,7},... | collective-permute-start | bytes 1572872 | tf_op jit(solution)/shard_map/ppermute | solution.py:25
  1.9 16.8 %collective-permute-start.3 = (bf16[512,512]{1,0:T(8,128)(2,1)}, bf16[512,512]{1,0:T(8,128)(2,1)S(1)}, u32[]{:S(2)}, u32[]{:S(2)}) collective-permute-start(bf16[512,512]{1,0:T(8,128)(2,1)} %nodes_ref.1), channel_id=1, source_target_pairs={{0,4},{2,6},{8,12},{10,14},{4,0},{6,2},{12,8},{14,10},{1,5},{3,7},... | collective-permute-start | bytes 1572872 | tf_op jit(solution)/shard_map/ppermute | solution.py:25
  3.2 20.8 %collective-permute-start.2 = (bf16[512,512]{1,0:T(8,128)(2,1)}, bf16[512,512]{1,0:T(8,128)(2,1)S(1)}, u32[]{:S(2)}, u32[]{:S(2)}) collective-permute-start(bf16[512,512]{1,0:T(8,128)(2,1)} %nodes_ref.1), channel_id=1, source_target_pairs={{4,8},{6,10},{8,4},{10,6},{5,9},{7,11},{9,5},{11,7},{20,24},{22,26... | collective-permute-start | bytes 1572872 | tf_op jit(solution)/shard_map/ppermute | solution.py:25
  8.8 20.6 %collective-permute-start.1 = (bf16[512,512]{1,0:T(8,128)(2,1)S(1)}, bf16[512,512]{1,0:T(8,128)(2,1)S(1)}, u32[]{:S(2)}, u32[]{:S(2)}) collective-permute-start(bf16[512,512]{1,0:T(8,128)(2,1)S(1)} %get-tuple-element.18.nodes_ref), channel_id=1, source_target_pairs={{2,4},{6,8},{10,12},{4,2},{8,6},{12,10},{3,5},{7,9},{11,13},{5,3},... | collective-permute-start | bytes 1572872 | tf_op jit(solution)/shard_map/ppermute | solution.py:25
  16.6 24.6 %collective-permute-start.5 = (bf16[512,512]{1,0:T(8,128)(2,1)S(1)}, bf16[512,512]{1,0:T(8,128)(2,1)S(1)}, u32[]{:S(2)}, u32[]{:S(2)}) collective-permute-start(bf16[512,512]{1,0:T(8,128)(2,1)S(1)} %tiles_1_0.1._), channel_id=1, source_target_pairs={{0,2},{4,6},{8,10},{12,14},{2,0},{6,4},{10,8},{14,12},{1,3},{5,7},... | collective-permute-start | bytes 1572872 | tf_op jit(solution)/shard_map/ppermute | solution.py:25
  20.1 21.4 %collective-permute-start.6 = (bf16[512,512]{1,0:T(8,128)(2,1)S(1)}, bf16[512,512]{1,0:T(8,128)(2,1)S(1)}, u32[]{:S(2)}, u32[]{:S(2)}) collective-permute-start(bf16[512,512]{1,0:T(8,128)(2,1)S(1)} %tiles_2_0.1._), channel_id=1, source_target_pairs={{0,4},{2,6},{8,12},{10,14},{4,0},{6,2},{12,8},{14,10},{1,5},{3,7},... | collective-permute-start | bytes 1572872 | tf_op jit(solution)/shard_map/ppermute | solution.py:25
  25.5 16.3 %collective-permute-start.7 = (bf16[512,512]{1,0:T(8,128)(2,1)S(1)}, bf16[512,512]{1,0:T(8,128)(2,1)S(1)}, u32[]{:S(2)}, u32[]{:S(2)}) collective-permute-start(bf16[512,512]{1,0:T(8,128)(2,1)S(1)} %tiles_2_1.1._), channel_id=1, source_target_pairs={{4,8},{6,10},{8,4},{10,6},{5,9},{7,11},{9,5},{11,7},{20,24},{22,26... | collective-permute-start | bytes 1572872 | tf_op jit(solution)/shard_map/ppermute | solution.py:25
  30.9 23.6 %collective-permute-start.8 = (bf16[512,512]{1,0:T(8,128)(2,1)S(1)}, bf16[512,512]{1,0:T(8,128)(2,1)S(1)}, u32[]{:S(2)}, u32[]{:S(2)}) collective-permute-start(bf16[512,512]{1,0:T(8,128)(2,1)S(1)} %tiles_1_1.1._), channel_id=1, source_target_pairs={{2,4},{6,8},{10,12},{4,2},{8,6},{12,10},{3,5},{7,9},{11,13},{5,3},... | collective-permute-start | bytes 1572872 | tf_op jit(solution)/shard_map/ppermute | solution.py:25
  41.5 13.0 %copy-start = (bf16[512,512]{1,0:T(8,128)(2,1)S(1)}, bf16[512,512]{1,0:T(8,128)(2,1)}, u32[]{:S(2)}) copy-start(bf16[512,512]{1,0:T(8,128)(2,1)} %nodes_ref.1) | copy-start | bytes 1572868
  41.5 13.0 %copy-start.1 = (bf16[512,512]{1,0:T(8,128)(2,1)S(1)}, bf16[512,512]{1,0:T(8,128)(2,1)}, u32[]{:S(2)}) copy-start(bf16[512,512]{1,0:T(8,128)(2,1)} %w_out_ref.1) | copy-start | bytes 1572868
  41.5 13.0 %copy-start.2 = (f32[512]{0:T(512)S(1)}, f32[512]{0:T(512)}, u32[]{:S(2)}) copy-start(f32[512]{0:T(512)} %param.17) | copy-start | bytes 6148

commit v3 on v2

--- a/solution.py
+++ b/solution.py
@@ -65,16 +65,18 @@
     pairs = key_ref.shape[1]
     wide = key_ref.shape[3]
     acc_ref[...] = jnp.zeros_like(acc_ref)
-    found = list_ref[code, 0]
-
-    def step(index, carry):
+    codes = list_ref.shape[0] // 2
+    found = list_ref[2 * codes, code]
+
+    def visit(first, count):
         tiles, gates = [], []
-        for u in range(UNROLL):
-            place = index * UNROLL + u
-            entry = list_ref[code, 1 + place]
+        for place in range(count):
+            place = first + place
+            entry, twin = list_ref[code, place], list_ref[codes + code, place]
             tile, source, target = entry & 1023, (entry >> 10) & 1023, entry >> 20
             half = jnp.where(place < found, 0.5, 0.0)
-            weight = (weight_ref[tile].astype(F32) * half).astype(BF16)
+            weight = weight_ref[tile].astype(F32) * half
+            weight += weight_ref[jnp.maximum(twin - 1, 0)].astype(F32) * jnp.where(twin > 0, half, 0.0)
             weight = jnp.concatenate([weight, weight], axis=1)
             target = pl.ds(pl.multiple_of(target * rows, rows), rows)
             tiles.append((source, target))
@@ -86,7 +88,7 @@
                     (((1,), (1,)), ((), ())),
                     preferred_element_type=F32,
                 )
-                gate.append(jnp.tanh(scores.astype(BF16)) * weight + weight)
+                gate.append((jnp.tanh(scores) * weight + weight).astype(BF16))
             gates.append(gate)
         sums = [
             [jnp.dot(gate[pair], value_ref[source, pair], preferred_element_type=F32) for pair in range(pairs)]
@@ -95,9 +97,16 @@
         for (_, target), total in zip(tiles, sums):
             for pair in range(pairs):
                 acc_ref[target, pair * wide : (pair + 1) * wide] += total[pair]
-        return carry
-
-    lax.fori_loop(0, pl.cdiv(found, UNROLL), step, 0)
+
+    many = found // (2 * UNROLL)
+
+    @pl.loop(0, many)
+    def _(index):
+        visit(index * (2 * UNROLL), 2 * UNROLL)
+
+    @pl.loop(2 * many, pl.cdiv(found, UNROLL))
+    def _(index):
+        visit(index * UNROLL, UNROLL)
 
 
 def start_copies(pairs, sems):
@@ -107,10 +116,40 @@
     return copies
 
 
+def make_lists(blocks, source, target, live, list_ref):
+    codes, tiles = list_ref.shape[0] // 2, source.shape[1]
+    square = (tiles, tiles)
+    down, along = lax.broadcasted_iota(jnp.int32, square, 0), lax.broadcasted_iota(jnp.int32, square, 1)
+    one = lambda mask: mask.astype(jnp.int32)
+    column = lambda row: jnp.sum(jnp.where(down == along, row, 0), axis=1, keepdims=True)
+    source_c, target_c = column(source), column(target)
+    code, code_c = target // blocks, target_c // blocks
+    number, number_c = along[:1], down[:, :1]
+    alike = (source == source_c) & (target == target_c)
+    rank = jnp.sum(one(alike & (down < along)), axis=0, keepdims=True)
+    rank_c = jnp.sum(one(alike & (along < down)), axis=1, keepdims=True)
+    first, first_c = (rank % 2 == 0) & (number < live), (rank_c % 2 == 0) & (number_c < live)
+    place_c = jnp.sum(one(first & (code == code_c) & (along < down)), axis=1, keepdims=True)
+    twin_c = jnp.sum(
+        jnp.where(alike & (rank == rank_c + 1) & (number < live), number + 1, 0), axis=1, keepdims=True
+    )
+    entry_c = number_c + source_c * 1024 + (target_c - code_c * blocks) * (1024 * 1024)
+    lane = lax.broadcasted_iota(jnp.int32, (tiles, list_ref.shape[1]), 1)
+    here = first_c & (place_c == lane)
+    lengths = jnp.zeros((1, list_ref.shape[1]), jnp.int32)
+    for each in range(codes):
+        mine = here & (code_c == each)
+        list_ref[each : each + 1] = jnp.sum(jnp.where(mine, entry_c, 0), axis=0, keepdims=True)
+        list_ref[codes + each : codes + each + 1] = jnp.sum(jnp.where(mine, twin_c, 0), axis=0, keepdims=True)
+        length = jnp.sum(one(first_c & (code_c == each)), axis=0, keepdims=True)
+        lengths += jnp.where(lane[:1] == each, length, 0)
+    list_ref[2 * codes :] = lengths
+
+
 def prepare_kernel(
     blocks, src_hbm, dst_hbm, nodes_hbm, gain_hbm, wk_hbm, wv_hbm, wq_hbm, weight_hbm, live_ref, other_ref,
-    key_ref, value_ref, weight_ref, nodes_ref, gain_ref, wq_ref, list_out,
-    wk_ref, wv_ref, src_ref, dst_ref, list_ref, sems,
+    key_ref, value_ref, weight_ref, query_ref, gain_ref, wq_ref, list_out,
+    nodes_ref, wk_ref, wv_ref, src_ref, dst_ref, sems,
 ):
     copies = start_copies(
         [
@@ -121,26 +160,7 @@
     )
     for copy in copies[:2]:
         copy.wait()
-    codes = list_ref.shape[0]
-    for code in range(codes):
-        list_ref[code, 0] = 0
-
-    def collect(tile, carry):
-        target = dst_ref[0, tile]
-        code = target // blocks
-        found = list_ref[code, 0] + 1
-        list_ref[code, found] = tile + src_ref[0, tile] * 1024 + (target - code * blocks) * (1024 * 1024)
-        list_ref[code, 0] = found
-        return carry
-
-    lax.fori_loop(0, live_ref[0, 0], collect, 0)
-    for code in range(codes):
-        found = list_ref[code, 0]
-        for extra in range(UNROLL):
-            list_ref[code, found + 1 + extra] = 0
-    list_copy = pltpu.make_async_copy(list_ref, list_out, sems.at[len(copies)])
-    list_copy.start()
-
+    make_lists(blocks, src_ref[...], dst_ref[...], live_ref[0, 0], list_out)
     me = lax.axis_index("col")
     copies[3].wait()
     other = rms_scale(other_ref[...], gain_ref[...]).astype(BF16)
@@ -153,22 +173,28 @@
     pack_heads(project(normed, wv_ref), value_ref, me * blocks)
     pack_heads(project(other, wv_ref), value_ref, (1 - me) * blocks)
     copies[6].wait()
+    query_ref[...] = scaled_query(normed, wq_ref)
     copies[7].wait()
-    list_copy.wait()
-
-
-def tiles_kernel(place, list_hbm, gain_ref, wq_ref, weight_ref, key_ref, value_ref, nodes_ref, _, out_ref, *scratch):
-    query_ref, list_ref, sem = scratch[:3]
+
+
+def tiles_kernel(places, list_hbm, gain_ref, wq_ref, weight_ref, key_ref, value_ref, *refs):
+    count = len(places)
+    block_refs, out_refs, (query_ref, acc_ref, list_ref, sem) = refs[:count], refs[count + 1 : 2 * count + 1], refs[2 * count + 1 :]
     copy = pltpu.make_async_copy(list_hbm, list_ref, sem)
     copy.start()
-    normed = rms_scale(nodes_ref[...], gain_ref[...]).astype(BF16)
-    query_ref[...] = scaled_query(normed, wq_ref)
-    copy.wait()
-    code = HALO + (partner_offset("row", *place) if place else 0)
-    sums = out_ref if out_ref.dtype == F32 else scratch[3]
-    visit_tiles(code, list_ref, weight_ref, query_ref, key_ref, value_ref, sums)
-    if out_ref.dtype != F32:
-        out_ref[...] = sums[...].astype(BF16)
+    for index, (place, block_ref, out_ref) in enumerate(zip(places, block_refs, out_refs)):
+        code, queries = HALO, block_ref
+        if place is not None:
+            code = HALO + partner_offset("row", *place)
+            if place != (1, 1):
+                queries = query_ref
+                query_ref[...] = scaled_query(rms_scale(block_ref[...], gain_ref[...]).astype(BF16), wq_ref)
+        if index == 0:
+            copy.wait()
+        sums = out_ref if out_ref.dtype == F32 else acc_ref
+        visit_tiles(code, list_ref, weight_ref, queries, key_ref, value_ref, sums)
+        if out_ref.dtype != F32:
+            out_ref[...] = sums[...].astype(BF16)
 
 
 def add_kernel(sum_ref, part_ref, out_ref):
@@ -198,27 +224,27 @@
     block_bf16 = shape((rows_dev, features), BF16)
     block_f32 = shape((rows_dev, features), F32)
     packed = shape((sources, pairs, 2 * tile_rows, wide), BF16)
-    lists = (codes, 1 + tile_count + UNROLL)
+    lists = (2 * codes + 1, 128)
+    assert tile_count + UNROLL <= 128 and sources <= 1024
     square = pltpu.VMEM((features, features), BF16)
 
     def in_hbm(*arrays):
         return [pltpu.with_memory_space_constraint(array, pltpu.HBM) for array in arrays]
 
-    places = ((1, 0), (2, 0), (2, 1), (1, 1))
+    groups = [((1, 0),), ((2, 1),), ((2, 0),), ((1, 1),)]
     other = lax.ppermute(nodes, "col", [(0, 1), (1, 0)])
-    arrived = {place: swap(nodes, "row", *place) for place in places[:3]}
-
-    keys, values, weight_held, nodes_held, gain, wq, lists_out = pl.pallas_call(
+    arrived = {place: swap(nodes, "row", *place) for group in groups for place in group if place != (1, 1)}
+    keys, values, weight_held, query, gain, wq, lists_out = pl.pallas_call(
         functools.partial(prepare_kernel, blocks),
         out_shape=(
             packed, packed, shape(weight.shape, BF16), block_bf16, shape((1, features), F32),
             shape(w_query.shape, BF16), shape(lists, jnp.int32),
         ),
         in_specs=[HBM] * 8 + [SMEM, VMEM],
-        out_specs=(VMEM,) * 6 + (HBM,),
+        out_specs=(VMEM,) * 7,
         scratch_shapes=[
-            square, square, pltpu.SMEM(tile_src.shape, jnp.int32), pltpu.SMEM(tile_dst.shape, jnp.int32),
-            pltpu.SMEM(lists, jnp.int32), pltpu.SemaphoreType.DMA((9,)),
+            pltpu.VMEM((rows_dev, features), BF16), square, square, pltpu.VMEM(tile_src.shape, jnp.int32),
+            pltpu.VMEM(tile_dst.shape, jnp.int32), pltpu.SemaphoreType.DMA((9,)),
         ],
         compiler_params=params,
         cost_estimate=cost,
@@ -228,27 +254,34 @@
         tile_live,
         other,
     )
-    arrived[places[3]] = swap(nodes_held, "row", *places[3])
-
-    def tiles(name, place, block, after, out):
+
+    arrived[1, 1] = swap(query, "row", 1, 1)
+
+    def tiles(name, places, blocks_in, after, out):
         return pl.pallas_call(
-            functools.partial(tiles_kernel, place),
-            out_shape=out,
-            in_specs=[HBM] + [VMEM] * 6 + [ANY],
-            out_specs=VMEM,
+            functools.partial(tiles_kernel, places),
+            out_shape=(out,) * len(places),
+            in_specs=[VMEM] * (6 + len(places)) + [ANY],
+            out_specs=(VMEM,) * len(places),
             scratch_shapes=[
-                pltpu.VMEM((rows_dev, features), BF16), pltpu.SMEM(lists, jnp.int32), pltpu.SemaphoreType.DMA,
-            ] + [pltpu.VMEM((rows_dev, features), F32)] * (out.dtype != F32),
+                pltpu.VMEM((rows_dev, features), BF16), pltpu.VMEM((rows_dev, features), F32),
+                pltpu.SMEM(lists, jnp.int32), pltpu.SemaphoreType.DMA,
+            ],
             compiler_params=params,
             cost_estimate=cost,
             name=name,
-        )(lists_out, gain, wq, weight_held, keys, values, block, after)
-
-    last, returned = gain, []
-    for place in places:
-        last = tiles("tiles_%d_%d" % place, place, arrived[place], last, block_bf16)
-        returned.append(swap(last, "row", *place))
-    total = tiles("own_tiles", None, nodes_held, last, block_f32)
+        )(lists_out, gain, wq, weight_held, keys, values, *blocks_in, after)
+
+    last, returned, total = gain, [], None
+    for index, group in enumerate(groups):
+        if index == 99:
+            (total,) = tiles("own_tiles", (None,), (query,), last, block_f32)
+            last = total
+        sums = tiles("tiles_%d" % index, group, [arrived[place] for place in group], last, block_bf16)
+        returned += [swap(part, "row", *place) for part, place in zip(sums, group)]
+        last = sums[-1]
+    if total is None:
+        (total,) = tiles("own_tiles", (None,), (query,), last, block_f32)
     for part in returned[:-1]:
         total = pl.pallas_call(
             add_kernel,

time: 55.5 us -> 54.3 us (0.978)
  the two profiles are of different devices: /device:TPU:21 before, /device:TPU:8 now
where the time goes in v3:
time: 54.3 us; the launch traced here: 54.1 us
  Pallas kernels  19.9 us (37%)
  starting transfers between devices  16.8 us (31%)
  waiting for transfers between devices  16.6 us (31%)
  between operations  0.82 us (2%)
    ppermute x8, starting transfers between devices, swap(): return lax.ppermute(block, axis, pairs + [(j, i) for i, j in pairs])  16.8 us
    ppermute x8, waiting for transfers between devices, swap(): return lax.ppermute(block, axis, pairs + [(j, i) for i, j in pairs])  16.6 us
    pallas_call x5, Pallas kernels, tiles(): pl.pallas_call(functools.partial(tiles_kernel, places), out_shape=(out,)...  14.4 us
    pallas_call x1, Pallas kernels, local(): pl.pallas_call(functools.partial(prepare_kernel, blocks), out_shape=(pack...  3.47 us
    pallas_call x1, Pallas kernels, local(): pl.pallas_call(last_kernel, out_shape=block_bf16, in_specs=[VMEM] * 5, ou...  1.34 us
  transfers between devices with their start and end apart: 9, of which 4 were waited for; matrix products, arithmetic and copies ran while one was open for 0% of the time, Pallas kernels for 34%

profile of v3, /device:TPU:8, one launch (start us, length us, event | category | flops | bytes accessed | tf_op | source)
XLA Modules:
  0.0 54.1 jit_solution(1818649398622163081)
XLA Ops:
  0.0 0.0 collective-permute-start
  0.0 1.5 %collective-permute-start.4 = (bf16[512,512]{1,0:T(8,128)(2,1)}, bf16[512,512]{1,0:T(8,128)(2,1)S(1)}, u32[]{:S(2)}, u32[]{:S(2)}) collective-permute-start(bf16[512,512]{1,0:T(8,128)(2,1)} %nodes_ref.1), channel_id=1, source_target_pairs={{0,2},{4,6},{8,10},{12,14},{2,0},{6,4},{10,8},{14,12},{1,3},{5,7},... | collective-permute-start | bytes 1572872 | tf_op jit(solution)/shard_map/ppermute | solution.py:25
  1.5 3.5 %collective-permute-start.3 = (bf16[512,512]{1,0:T(8,128)(2,1)}, bf16[512,512]{1,0:T(8,128)(2,1)S(1)}, u32[]{:S(2)}, u32[]{:S(2)}) collective-permute-start(bf16[512,512]{1,0:T(8,128)(2,1)} %nodes_ref.1), channel_id=1, source_target_pairs={{4,8},{6,10},{8,4},{10,6},{5,9},{7,11},{9,5},{11,7},{20,24},{22,26... | collective-permute-start | bytes 1572872 | tf_op jit(solution)/shard_map/ppermute | solution.py:25
  5.0 0.1 collective-permute-start.2
  5.7 0.0 collective-permute-done.other_ref
  5.7 3.5 %prepare.1 = (bf16[8,4,256,128]{3,2,1,0:T(8,128)(2,1)S(1)}, bf16[8,4,256,128]{3,2,1,0:T(8,128)(2,1)S(1)}, bf16[64,128,128]{2,1,0:T(8,128)(2,1)S(1)}, bf16[512,51...) custom-call(s32[1,64]{1,0:T(1,128)} %src_hbm.1, ...), custom_call_target="tpu_custom_call" | custom-call | flops 1048576 | bytes 65536 | tf_op jit(solution)/shard_map/prepare/pallas_call | solution.py:237
  9.2 3.9 %collective-permute-start.1 = (bf16[512,512]{1,0:T(8,128)(2,1)S(1)}, bf16[512,512]{1,0:T(8,128)(2,1)S(1)}, u32[]{:S(2)}, u32[]{:S(2)}) collective-permute-start(bf16[512,512]{1,0:T(8,128)(2,1)S(1)} %get-tuple-element.18.refs_0_), channel_id=1, source_target_pairs={{2,4},{6,8},{10,12},{4,2},{8,6},{12,10},{3,5},{7,9},{11,13},{5,3},... | collective-permute-start | bytes 1572872 | tf_op jit(solution)/shard_map/ppermute | solution.py:25
  13.1 1.5 %collective-permute-done.4.refs_0_ = bf16[512,512]{1,0:T(8,128)(2,1)S(1)} collective-permute-done((bf16[512,512]{1,0:T(8,128)(2,1)}, bf16[512,512]{1,0:T(8,128)(2,1)S(1)}, u32[]{:S(2)}, u32[]{:S(2)}) %collective-permute-start.4) | collective-permute-done | bytes 524320 | tf_op jit(solution)/shard_map/ppermute | solution.py:25
  14.6 3.0 %tiles_0.1.refs_1_ = bf16[512,512]{1,0:T(8,128)(2,1)S(1)} custom-call(s32[11,128]{1,0:T(8,128)S(1)} %get-tuple-element.12.list_hbm, f32[1,512]{1,0:T(1,128)S(1)} %get-tuple-element.13.gain_ref.refs_1_, bf16[512,512]{1,0:T(8,128)(2,1)S(1)} %get-tuple-element.14.wq_ref, bf16[64,128,128]{2,1,0:T(8,128)(2,1)S(1)} %get-tuple-element.15.weight_ref, ...), custom_call_target="tpu_custom_call" | custom-call | flops 1048576 | bytes 65536 | tf_op jit(solution)/shard_map/tiles_0/pallas_call | solution.py:261
  17.6 0.9 %collective-permute-start.5 = (bf16[512,512]{1,0:T(8,128)(2,1)S(1)}, bf16[512,512]{1,0:T(8,128)(2,1)S(1)}, u32[]{:S(2)}, u32[]{:S(2)}) collective-permute-start(bf16[512,512]{1,0:T(8,128)(2,1)S(1)} %tiles_0.1.refs_1_), channel_id=1, source_target_pairs={{0,2},{4,6},{8,10},{12,14},{2,0},{6,4},{10,8},{14,12},{1,3},{5,7},... | collective-permute-start | bytes 1572872 | tf_op jit(solution)/shard_map/ppermute | solution.py:25
  18.5 0.0 collective-permute-done.3.refs_0_
  18.5 3.0 %tiles_1.1.refs_1_ = bf16[512,512]{1,0:T(8,128)(2,1)S(1)} custom-call(s32[11,128]{1,0:T(8,128)S(1)} %get-tuple-element.12.list_hbm, f32[1,512]{1,0:T(1,128)S(1)} %get-tuple-element.13.gain_ref.refs_1_, bf16[512,512]{1,0:T(8,128)(2,1)S(1)} %get-tuple-element.14.wq_ref, bf16[64,128,128]{2,1,0:T(8,128)(2,1)S(1)} %get-tuple-element.15.weight_ref, ...), custom_call_target="tpu_custom_call" | custom-call | flops 1048576 | bytes 65536 | tf_op jit(solution)/shard_map/tiles_1/pallas_call | solution.py:261
  21.5 4.9 %collective-permute-start.6 = (bf16[512,512]{1,0:T(8,128)(2,1)S(1)}, bf16[512,512]{1,0:T(8,128)(2,1)S(1)}, u32[]{:S(2)}, u32[]{:S(2)}) collective-permute-start(bf16[512,512]{1,0:T(8,128)(2,1)S(1)} %tiles_1.1.refs_1_), channel_id=1, source_target_pairs={{4,8},{6,10},{8,4},{10,6},{5,9},{7,11},{9,5},{11,7},{20,24},{22,26... | collective-permute-start | bytes 1572872 | tf_op jit(solution)/shard_map/ppermute | solution.py:25
  26.4 0.0 collective-permute-done.2.refs_0_
  26.4 3.0 %tiles_2.1.refs_1_ = bf16[512,512]{1,0:T(8,128)(2,1)S(1)} custom-call(s32[11,128]{1,0:T(8,128)S(1)} %get-tuple-element.12.list_hbm, f32[1,512]{1,0:T(1,128)S(1)} %get-tuple-element.13.gain_ref.refs_1_, bf16[512,512]{1,0:T(8,128)(2,1)S(1)} %get-tuple-element.14.wq_ref, bf16[64,128,128]{2,1,0:T(8,128)(2,1)S(1)} %get-tuple-element.15.weight_ref, ...), custom_call_target="tpu_custom_call" | custom-call | flops 1048576 | bytes 65536 | tf_op jit(solution)/shard_map/tiles_2/pallas_call | solution.py:261
  29.5 0.1 collective-permute-start.7
  29.5 1.3 %collective-permute-done.1.refs_0_ = bf16[512,512]{1,0:T(8,128)(2,1)S(1)} collective-permute-done((bf16[512,512]{1,0:T(8,128)(2,1)S(1)}, bf16[512,512]{1,0:T(8,128)(2,1)S(1)}, u32[]{:S(2)}, u32[]{:S(2)}) %collective-permute-start.1) | collective-permute-done | bytes 524320 | tf_op jit(solution)/shard_map/ppermute | solution.py:25
  30.8 3.1 %tiles_3.1.refs_1_ = bf16[512,512]{1,0:T(8,128)(2,1)S(1)} custom-call(s32[11,128]{1,0:T(8,128)S(1)} %get-tuple-element.12.list_hbm, f32[1,512]{1,0:T(1,128)S(1)} %get-tuple-element.13.gain_ref.refs_1_, bf16[512,512]{1,0:T(8,128)(2,1)S(1)} %get-tuple-element.14.wq_ref, bf16[64,128,128]{2,1,0:T(8,128)(2,1)S(1)} %get-tuple-element.15.weight_ref, ...), custom_call_target="tpu_custom_call" | custom-call | flops 1048576 | bytes 65536 | tf_op jit(solution)/shard_map/tiles_3/pallas_call | solution.py:261
  34.0 1.9 %collective-permute-start.8 = (bf16[512,512]{1,0:T(8,128)(2,1)S(1)}, bf16[512,512]{1,0:T(8,128)(2,1)S(1)}, u32[]{:S(2)}, u32[]{:S(2)}) collective-permute-start(bf16[512,512]{1,0:T(8,128)(2,1)S(1)} %tiles_3.1.refs_1_), channel_id=1, source_target_pairs={{2,4},{6,8},{10,12},{4,2},{8,6},{12,10},{3,5},{7,9},{11,13},{5,3},... | collective-permute-start | bytes 1572872 | tf_op jit(solution)/shard_map/ppermute | solution.py:25
  35.9 2.3 %own_tiles.1.sum_ref = f32[512,512]{1,0:T(8,128)S(1)} custom-call(s32[11,128]{1,0:T(8,128)S(1)} %get-tuple-element.12.list_hbm, f32[1,512]{1,0:T(1,128)S(1)} %get-tuple-element.13.gain_ref.refs_1_, bf16[512,512]{1,0:T(8,128)(2,1)S(1)} %get-tuple-element.14.wq_ref, bf16[64,128,128]{2,1,0:T(8,128)(2,1)S(1)} %get-tuple-element.15.weight_ref, ...), custom_call_target="tpu_custom_call" | custom-call | flops 1048576 | bytes 65536 | tf_op jit(solution)/shard_map/own_tiles/pallas_call | solution.py:261
  38.2 3.4 %collective-permute-done.5.part_ref = bf16[512,512]{1,0:T(8,128)(2,1)S(1)} collective-permute-done((bf16[512,512]{1,0:T(8,128)(2,1)S(1)}, bf16[512,512]{1,0:T(8,128)(2,1)S(1)}, u32[]{:S(2)}, u32[]{:S(2)}) %collective-permute-start.5) | collective-permute-done | bytes 524320 | tf_op jit(solution)/shard_map/ppermute | solution.py:25
  41.6 0.2 add.3.sum_ref
  41.8 0.0 copy-start
  41.8 0.0 copy-start.1
  41.8 0.0 copy-start.2
  41.8 0.0 collective-permute-done.6.part_ref
  41.8 0.2 add.4.sum_ref
  42.0 0.0 collective-permute-done.7.part_ref
  42.1 0.2 add.5.sum_ref
  42.3 10.5 %collective-permute-done.8.part_ref = bf16[512,512]{1,0:T(8,128)(2,1)S(1)} collective-permute-done((bf16[512,512]{1,0:T(8,128)(2,1)S(1)}, bf16[512,512]{1,0:T(8,128)(2,1)S(1)}, u32[]{:S(2)}, u32[]{:S(2)}) %collective-permute-start.8) | collective-permute-done | bytes 524320 | tf_op jit(solution)/shard_map/ppermute | solution.py:25
  52.8 0.0 copy-done
  52.8 0.0 copy-done.1
  52.8 0.0 copy-done.2
  52.8 1.3 %mix.1 = bf16[512,512]{1,0:T(8,128)(2,1)} custom-call(bf16[512,512]{1,0:T(8,128)(2,1)S(1)} %copy-done, f32[1,512]{1,0:T(1,128)S(1)} %bitcast.3, bf16[512,512]{1,0:T(8,128)(2,1)S(1)} %copy-done.1, f32[512,512]{1,0:T(8,128)S(1)} %add.5.sum_ref, bf16[512,512]{1,0:T(8,128)(2,1)S(1)} %collective-permute-done.8.part_ref), custom_call_target="tpu_custom_call" | custom-call | flops 1048576 | bytes 65536 | tf_op jit(solution)/shard_map/mix/pallas_call | solution.py:297
Async XLA Ops:
  0.0 5.7 %collective-permute-start = (bf16[512,512]{1,0:T(8,128)(2,1)}, bf16[512,512]{1,0:T(8,128)(2,1)S(1)}, u32[]{:S(2)}, u32[]{:S(2)}) collective-permute-start(bf16[512,512]{1,0:T(8,128)(2,1)} %nodes_ref.1), channel_id=1, source_target_pairs={{0,1},{1,0},{2,3},{3,2},{4,5},{5,4},{6,7},{7,6},{8,9},{9,8},{10,11... | collective-permute-start | bytes 1572872 | tf_op jit(solution)/shard_map/ppermute | solution.py:235
  0.0 14.5 %collective-permute-start.4 = (bf16[512,512]{1,0:T(8,128)(2,1)}, bf16[512,512]{1,0:T(8,128)(2,1)S(1)}, u32[]{:S(2)}, u32[]{:S(2)}) collective-permute-start(bf16[512,512]{1,0:T(8,128)(2,1)} %nodes_ref.1), channel_id=1, source_target_pairs={{0,2},{4,6},{8,10},{12,14},{2,0},{6,4},{10,8},{14,12},{1,3},{5,7},... | collective-permute-start | bytes 1572872 | tf_op jit(solution)/shard_map/ppermute | solution.py:25
  1.5 17.0 %collective-permute-start.3 = (bf16[512,512]{1,0:T(8,128)(2,1)}, bf16[512,512]{1,0:T(8,128)(2,1)S(1)}, u32[]{:S(2)}, u32[]{:S(2)}) collective-permute-start(bf16[512,512]{1,0:T(8,128)(2,1)} %nodes_ref.1), channel_id=1, source_target_pairs={{4,8},{6,10},{8,4},{10,6},{5,9},{7,11},{9,5},{11,7},{20,24},{22,26... | collective-permute-start | bytes 1572872 | tf_op jit(solution)/shard_map/ppermute | solution.py:25
  5.0 21.5 %collective-permute-start.2 = (bf16[512,512]{1,0:T(8,128)(2,1)}, bf16[512,512]{1,0:T(8,128)(2,1)S(1)}, u32[]{:S(2)}, u32[]{:S(2)}) collective-permute-start(bf16[512,512]{1,0:T(8,128)(2,1)} %nodes_ref.1), channel_id=1, source_target_pairs={{0,4},{2,6},{8,12},{10,14},{4,0},{6,2},{12,8},{14,10},{1,5},{3,7},... | collective-permute-start | bytes 1572872 | tf_op jit(solution)/shard_map/ppermute | solution.py:25
  9.2 21.6 %collective-permute-start.1 = (bf16[512,512]{1,0:T(8,128)(2,1)S(1)}, bf16[512,512]{1,0:T(8,128)(2,1)S(1)}, u32[]{:S(2)}, u32[]{:S(2)}) collective-permute-start(bf16[512,512]{1,0:T(8,128)(2,1)S(1)} %get-tuple-element.18.refs_0_), channel_id=1, source_target_pairs={{2,4},{6,8},{10,12},{4,2},{8,6},{12,10},{3,5},{7,9},{11,13},{5,3},... | collective-permute-start | bytes 1572872 | tf_op jit(solution)/shard_map/ppermute | solution.py:25
  17.6 24.0 %collective-permute-start.5 = (bf16[512,512]{1,0:T(8,128)(2,1)S(1)}, bf16[512,512]{1,0:T(8,128)(2,1)S(1)}, u32[]{:S(2)}, u32[]{:S(2)}) collective-permute-start(bf16[512,512]{1,0:T(8,128)(2,1)S(1)} %tiles_0.1.refs_1_), channel_id=1, source_target_pairs={{0,2},{4,6},{8,10},{12,14},{2,0},{6,4},{10,8},{14,12},{1,3},{5,7},... | collective-permute-start | bytes 1572872 | tf_op jit(solution)/shard_map/ppermute | solution.py:25
  21.5 20.3 %collective-permute-start.6 = (bf16[512,512]{1,0:T(8,128)(2,1)S(1)}, bf16[512,512]{1,0:T(8,128)(2,1)S(1)}, u32[]{:S(2)}, u32[]{:S(2)}) collective-permute-start(bf16[512,512]{1,0:T(8,128)(2,1)S(1)} %tiles_1.1.refs_1_), channel_id=1, source_target_pairs={{4,8},{6,10},{8,4},{10,6},{5,9},{7,11},{9,5},{11,7},{20,24},{22,26... | collective-permute-start | bytes 1572872 | tf_op jit(solution)/shard_map/ppermute | solution.py:25
  29.5 12.6 %collective-permute-start.7 = (bf16[512,512]{1,0:T(8,128)(2,1)S(1)}, bf16[512,512]{1,0:T(8,128)(2,1)S(1)}, u32[]{:S(2)}, u32[]{:S(2)}) collective-permute-start(bf16[512,512]{1,0:T(8,128)(2,1)S(1)} %tiles_2.1.refs_1_), channel_id=1, source_target_pairs={{0,4},{2,6},{8,12},{10,14},{4,0},{6,2},{12,8},{14,10},{1,5},{3,7},... | collective-permute-start | bytes 1572872 | tf_op jit(solution)/shard_map/ppermute | solution.py:25
  34.0 18.8 %collective-permute-start.8 = (bf16[512,512]{1,0:T(8,128)(2,1)S(1)}, bf16[512,512]{1,0:T(8,128)(2,1)S(1)}, u32[]{:S(2)}, u32[]{:S(2)}) collective-permute-start(bf16[512,512]{1,0:T(8,128)(2,1)S(1)} %tiles_3.1.refs_1_), channel_id=1, source_target_pairs={{2,4},{6,8},{10,12},{4,2},{8,6},{12,10},{3,5},{7,9},{11,13},{5,3},... | collective-permute-start | bytes 1572872 | tf_op jit(solution)/shard_map/ppermute | solution.py:25
  41.8 11.0 %copy-start = (bf16[512,512]{1,0:T(8,128)(2,1)S(1)}, bf16[512,512]{1,0:T(8,128)(2,1)}, u32[]{:S(2)}) copy-start(bf16[512,512]{1,0:T(8,128)(2,1)} %nodes_ref.1) | copy-start | bytes 1572868
  41.8 11.0 %copy-start.1 = (bf16[512,512]{1,0:T(8,128)(2,1)S(1)}, bf16[512,512]{1,0:T(8,128)(2,1)}, u32[]{:S(2)}) copy-start(bf16[512,512]{1,0:T(8,128)(2,1)} %w_out_ref.1) | copy-start | bytes 1572868
  41.8 10.9 %copy-start.2 = (f32[512]{0:T(512)S(1)}, f32[512]{0:T(512)}, u32[]{:S(2)}) copy-start(f32[512]{0:T(512)} %param.17) | copy-start | bytes 6148

commit v4 on v3

--- a/solution.py
+++ b/solution.py
@@ -177,24 +177,22 @@
     copies[7].wait()
 
 
-def tiles_kernel(places, list_hbm, gain_ref, wq_ref, weight_ref, key_ref, value_ref, *refs):
-    count = len(places)
-    block_refs, out_refs, (query_ref, acc_ref, list_ref, sem) = refs[:count], refs[count + 1 : 2 * count + 1], refs[2 * count + 1 :]
-    copy = pltpu.make_async_copy(list_hbm, list_ref, sem)
+def tiles_kernel(
+    place, projected, lists_vmem, gain_ref, wq_ref, weight_ref, key_ref, value_ref, block_ref, _, out_ref,
+    query_ref, acc_ref, list_ref, sem,
+):
+    copy = pltpu.make_async_copy(lists_vmem, list_ref, sem)
     copy.start()
-    for index, (place, block_ref, out_ref) in enumerate(zip(places, block_refs, out_refs)):
-        code, queries = HALO, block_ref
-        if place is not None:
-            code = HALO + partner_offset("row", *place)
-            if place != (1, 1):
-                queries = query_ref
-                query_ref[...] = scaled_query(rms_scale(block_ref[...], gain_ref[...]).astype(BF16), wq_ref)
-        if index == 0:
-            copy.wait()
-        sums = out_ref if out_ref.dtype == F32 else acc_ref
-        visit_tiles(code, list_ref, weight_ref, queries, key_ref, value_ref, sums)
-        if out_ref.dtype != F32:
-            out_ref[...] = sums[...].astype(BF16)
+    queries = block_ref
+    if not projected:
+        queries = query_ref
+        query_ref[...] = scaled_query(rms_scale(block_ref[...], gain_ref[...]).astype(BF16), wq_ref)
+    copy.wait()
+    code = HALO + (partner_offset("row", *place) if place else 0)
+    sums = out_ref if out_ref.dtype == F32 else acc_ref
+    visit_tiles(code, list_ref, weight_ref, queries, key_ref, value_ref, sums)
+    if out_ref.dtype != F32:
+        out_ref[...] = sums[...].astype(BF16)
 
 
 def add_kernel(sum_ref, part_ref, out_ref):
@@ -231,9 +229,11 @@
     def in_hbm(*arrays):
         return [pltpu.with_memory_space_constraint(array, pltpu.HBM) for array in arrays]
 
-    groups = [((1, 0),), ((2, 1),), ((2, 0),), ((1, 1),)]
+    near, diagonal = (1, 0), (1, 1)
+    places = (near, (HALO, 1), (HALO, 0), diagonal)
     other = lax.ppermute(nodes, "col", [(0, 1), (1, 0)])
-    arrived = {place: swap(nodes, "row", *place) for group in groups for place in group if place != (1, 1)}
+    arrived = {place: swap(nodes, "row", *place) for place in places if place != diagonal}
+
     keys, values, weight_held, query, gain, wq, lists_out = pl.pallas_call(
         functools.partial(prepare_kernel, blocks),
         out_shape=(
@@ -255,14 +255,14 @@
         other,
     )
 
-    arrived[1, 1] = swap(query, "row", 1, 1)
-
-    def tiles(name, places, blocks_in, after, out):
+    arrived[diagonal] = swap(query, "row", *diagonal)
+
+    def tiles(name, place, projected, block, after, out):
         return pl.pallas_call(
-            functools.partial(tiles_kernel, places),
-            out_shape=(out,) * len(places),
-            in_specs=[VMEM] * (6 + len(places)) + [ANY],
-            out_specs=(VMEM,) * len(places),
+            functools.partial(tiles_kernel, place, projected),
+            out_shape=out,
+            in_specs=[VMEM] * 7 + [ANY],
+            out_specs=VMEM,
             scratch_shapes=[
                 pltpu.VMEM((rows_dev, features), BF16), pltpu.VMEM((rows_dev, features), F32),
                 pltpu.SMEM(lists, jnp.int32), pltpu.SemaphoreType.DMA,
@@ -270,18 +270,13 @@
             compiler_params=params,
             cost_estimate=cost,
             name=name,
-        )(lists_out, gain, wq, weight_held, keys, values, *blocks_in, after)
-
-    last, returned, total = gain, [], None
-    for index, group in enumerate(groups):
-        if index == 99:
-            (total,) = tiles("own_tiles", (None,), (query,), last, block_f32)
-            last = total
-        sums = tiles("tiles_%d" % index, group, [arrived[place] for place in group], last, block_bf16)
-        returned += [swap(part, "row", *place) for part, place in zip(sums, group)]
-        last = sums[-1]
-    if total is None:
-        (total,) = tiles("own_tiles", (None,), (query,), last, block_f32)
+        )(lists_out, gain, wq, weight_held, keys, values, block, after)
+
+    last, returned = gain, []
+    for place in places:
+        last = tiles("tiles_%d_%d" % place, place, place == diagonal, arrived[place], last, block_bf16)
+        returned.append(swap(last, "row", *place))
+    total = tiles("own_tiles", None, True, query, last, block_f32)
     for part in returned[:-1]:
         total = pl.pallas_call(
             add_kernel,

time: 54.3 us -> 54.3 us (level)
  Pallas kernels: 19.9 us -> 16.2 us
  starting transfers between devices: 16.8 us -> 18.9 us
  waiting for transfers between devices: 16.6 us -> 18.2 us
    pallas_call x5, Pallas kernels: 14.4 us -> 10.8 us  [tiles(): pl.pallas_call(functools.partial(tiles_kernel, place, projected), out_sha...]
    ppermute x8, starting transfers between devices: 16.8 us -> 18.9 us  [swap(): return lax.ppermute(block, axis, pairs + [(j, i) for i, j in pairs])]
    ppermute x8, waiting for transfers between devices: 16.6 us -> 18.2 us  [swap(): return lax.ppermute(block, axis, pairs + [(j, i) for i, j in pairs])]
  transfers between devices with their start and end apart: 9 -> 9, of which waited for: 4 -> 5; matrix products, arithmetic and copies ran while one was open for 0% -> 0% of each run, Pallas kernels for 34% -> 27%
where the time goes in v4:
time: 54.3 us; the launch traced here: 54.1 us
  starting transfers between devices  18.9 us (35%)
  waiting for transfers between devices  18.2 us (34%)
  Pallas kernels  16.2 us (30%)
  between operations  0.82 us (2%)
    ppermute x8, starting transfers between devices, swap(): return lax.ppermute(block, axis, pairs + [(j, i) for i, j in pairs])  18.9 us
    ppermute x8, waiting for transfers between devices, swap(): return lax.ppermute(block, axis, pairs + [(j, i) for i, j in pairs])  18.2 us
    pallas_call x5, Pallas kernels, tiles(): pl.pallas_call(functools.partial(tiles_kernel, place, projected), out_sha...  10.8 us
    pallas_call x1, Pallas kernels, local(): pl.pallas_call(functools.partial(prepare_kernel, blocks), out_shape=(pack...  3.47 us
    pallas_call x1, Pallas kernels, local(): pl.pallas_call(last_kernel, out_shape=block_bf16, in_specs=[VMEM] * 5, ou...  1.34 us
  transfers between devices with their start and end apart: 9, of which 5 were waited for; matrix products, arithmetic and copies ran while one was open for 0% of the time, Pallas kernels for 27%

profile of v4, /device:TPU:8, one launch (start us, length us, event | category | flops | bytes accessed | tf_op | source)
XLA Modules:
  0.0 54.1 jit_solution(5133981824939796167)
XLA Ops:
  0.0 0.0 collective-permute-start
  0.0 1.5 %collective-permute-start.4 = (bf16[512,512]{1,0:T(8,128)(2,1)}, bf16[512,512]{1,0:T(8,128)(2,1)S(1)}, u32[]{:S(2)}, u32[]{:S(2)}) collective-permute-start(bf16[512,512]{1,0:T(8,128)(2,1)} %nodes_ref.1), channel_id=1, source_target_pairs={{0,2},{4,6},{8,10},{12,14},{2,0},{6,4},{10,8},{14,12},{1,3},{5,7},... | collective-permute-start | bytes 1572872 | tf_op jit(solution)/shard_map/ppermute | solution.py:25
  1.5 3.5 %collective-permute-start.3 = (bf16[512,512]{1,0:T(8,128)(2,1)}, bf16[512,512]{1,0:T(8,128)(2,1)S(1)}, u32[]{:S(2)}, u32[]{:S(2)}) collective-permute-start(bf16[512,512]{1,0:T(8,128)(2,1)} %nodes_ref.1), channel_id=1, source_target_pairs={{4,8},{6,10},{8,4},{10,6},{5,9},{7,11},{9,5},{11,7},{20,24},{22,26... | collective-permute-start | bytes 1572872 | tf_op jit(solution)/shard_map/ppermute | solution.py:25
  5.0 0.1 collective-permute-start.2
  5.7 0.0 collective-permute-done.other_ref
  5.7 3.5 %prepare.1 = (bf16[8,4,256,128]{3,2,1,0:T(8,128)(2,1)S(1)}, bf16[8,4,256,128]{3,2,1,0:T(8,128)(2,1)S(1)}, bf16[64,128,128]{2,1,0:T(8,128)(2,1)S(1)}, bf16[512,51...) custom-call(s32[1,64]{1,0:T(1,128)} %src_hbm.1, ...), custom_call_target="tpu_custom_call" | custom-call | flops 1048576 | bytes 65536 | tf_op jit(solution)/shard_map/prepare/pallas_call | solution.py:237
  9.2 3.9 %collective-permute-start.1 = (bf16[512,512]{1,0:T(8,128)(2,1)S(1)}, bf16[512,512]{1,0:T(8,128)(2,1)S(1)}, u32[]{:S(2)}, u32[]{:S(2)}) collective-permute-start(bf16[512,512]{1,0:T(8,128)(2,1)S(1)} %get-tuple-element.18.block_ref), channel_id=1, source_target_pairs={{2,4},{6,8},{10,12},{4,2},{8,6},{12,10},{3,5},{7,9},{11,13},{5,3},... | collective-permute-start | bytes 1572872 | tf_op jit(solution)/shard_map/ppermute | solution.py:25
  13.1 1.5 %collective-permute-done.4.block_ref = bf16[512,512]{1,0:T(8,128)(2,1)S(1)} collective-permute-done((bf16[512,512]{1,0:T(8,128)(2,1)}, bf16[512,512]{1,0:T(8,128)(2,1)S(1)}, u32[]{:S(2)}, u32[]{:S(2)}) %collective-permute-start.4) | collective-permute-done | bytes 524320 | tf_op jit(solution)/shard_map/ppermute | solution.py:25
  14.6 1.6 %tiles_1_0.1._ = bf16[512,512]{1,0:T(8,128)(2,1)S(1)} custom-call(s32[11,128]{1,0:T(8,128)S(1)} %get-tuple-element.12.lists_vmem, f32[1,512]{1,0:T(1,128)S(1)} %get-tuple-element.13.gain_ref._, bf16[512,512]{1,0:T(8,128)(2,1)S(1)} %get-tuple-element.14.wq_ref, bf16[64,128,128]{2,1,0:T(8,128)(2,1)S(1)} %get-tuple-element.15.weight_ref, ...), custom_call_target="tpu_custom_call" | custom-call | flops 1048576 | bytes 65536 | tf_op jit(solution)/shard_map/tiles_1_0/pallas_call | solution.py:261
  16.1 1.6 %collective-permute-start.5 = (bf16[512,512]{1,0:T(8,128)(2,1)S(1)}, bf16[512,512]{1,0:T(8,128)(2,1)S(1)}, u32[]{:S(2)}, u32[]{:S(2)}) collective-permute-start(bf16[512,512]{1,0:T(8,128)(2,1)S(1)} %tiles_1_0.1._), channel_id=1, source_target_pairs={{0,2},{4,6},{8,10},{12,14},{2,0},{6,4},{10,8},{14,12},{1,3},{5,7},... | collective-permute-start | bytes 1572872 | tf_op jit(solution)/shard_map/ppermute | solution.py:25
  17.7 0.7 %collective-permute-done.3.block_ref = bf16[512,512]{1,0:T(8,128)(2,1)S(1)} collective-permute-done((bf16[512,512]{1,0:T(8,128)(2,1)}, bf16[512,512]{1,0:T(8,128)(2,1)S(1)}, u32[]{:S(2)}, u32[]{:S(2)}) %collective-permute-start.3) | collective-permute-done | bytes 524320 | tf_op jit(solution)/shard_map/ppermute | solution.py:25
  18.3 2.2 %tiles_2_1.1._ = bf16[512,512]{1,0:T(8,128)(2,1)S(1)} custom-call(s32[11,128]{1,0:T(8,128)S(1)} %get-tuple-element.12.lists_vmem, f32[1,512]{1,0:T(1,128)S(1)} %get-tuple-element.13.gain_ref._, bf16[512,512]{1,0:T(8,128)(2,1)S(1)} %get-tuple-element.14.wq_ref, bf16[64,128,128]{2,1,0:T(8,128)(2,1)S(1)} %get-tuple-element.15.weight_ref, ...), custom_call_target="tpu_custom_call" | custom-call | flops 1048576 | bytes 65536 | tf_op jit(solution)/shard_map/tiles_2_1/pallas_call | solution.py:261
  20.6 4.4 %collective-permute-start.6 = (bf16[512,512]{1,0:T(8,128)(2,1)S(1)}, bf16[512,512]{1,0:T(8,128)(2,1)S(1)}, u32[]{:S(2)}, u32[]{:S(2)}) collective-permute-start(bf16[512,512]{1,0:T(8,128)(2,1)S(1)} %tiles_2_1.1._), channel_id=1, source_target_pairs={{4,8},{6,10},{8,4},{10,6},{5,9},{7,11},{9,5},{11,7},{20,24},{22,26... | collective-permute-start | bytes 1572872 | tf_op jit(solution)/shard_map/ppermute | solution.py:25
  25.0 0.0 collective-permute-done.2.block_ref
  25.0 2.4 %tiles_2_0.1._ = bf16[512,512]{1,0:T(8,128)(2,1)S(1)} custom-call(s32[11,128]{1,0:T(8,128)S(1)} %get-tuple-element.12.lists_vmem, f32[1,512]{1,0:T(1,128)S(1)} %get-tuple-element.13.gain_ref._, bf16[512,512]{1,0:T(8,128)(2,1)S(1)} %get-tuple-element.14.wq_ref, bf16[64,128,128]{2,1,0:T(8,128)(2,1)S(1)} %get-tuple-element.15.weight_ref, ...), custom_call_target="tpu_custom_call" | custom-call | flops 1048576 | bytes 65536 | tf_op jit(solution)/shard_map/tiles_2_0/pallas_call | solution.py:261
  27.3 0.1 collective-permute-start.7
  27.4 3.9 %collective-permute-done.1.block_ref = bf16[512,512]{1,0:T(8,128)(2,1)S(1)} collective-permute-done((bf16[512,512]{1,0:T(8,128)(2,1)S(1)}, bf16[512,512]{1,0:T(8,128)(2,1)S(1)}, u32[]{:S(2)}, u32[]{:S(2)}) %collective-permute-start.1) | collective-permute-done | bytes 524320 | tf_op jit(solution)/shard_map/ppermute | solution.py:25
  31.3 1.7 %tiles_1_1.1._ = bf16[512,512]{1,0:T(8,128)(2,1)S(1)} custom-call(s32[11,128]{1,0:T(8,128)S(1)} %get-tuple-element.12.lists_vmem, f32[1,512]{1,0:T(1,128)S(1)} %get-tuple-element.13.gain_ref._, bf16[512,512]{1,0:T(8,128)(2,1)S(1)} %get-tuple-element.14.wq_ref, bf16[64,128,128]{2,1,0:T(8,128)(2,1)S(1)} %get-tuple-element.15.weight_ref, ...), custom_call_target="tpu_custom_call" | custom-call | flops 1048576 | bytes 65536 | tf_op jit(solution)/shard_map/tiles_1_1/pallas_call | solution.py:261
  33.0 3.9 %collective-permute-start.8 = (bf16[512,512]{1,0:T(8,128)(2,1)S(1)}, bf16[512,512]{1,0:T(8,128)(2,1)S(1)}, u32[]{:S(2)}, u32[]{:S(2)}) collective-permute-start(bf16[512,512]{1,0:T(8,128)(2,1)S(1)} %tiles_1_1.1._), channel_id=1, source_target_pairs={{2,4},{6,8},{10,12},{4,2},{8,6},{12,10},{3,5},{7,9},{11,13},{5,3},... | collective-permute-start | bytes 1572872 | tf_op jit(solution)/shard_map/ppermute | solution.py:25
  37.0 3.0 %own_tiles.1.sum_ref = f32[512,512]{1,0:T(8,128)S(1)} custom-call(s32[11,128]{1,0:T(8,128)S(1)} %get-tuple-element.12.lists_vmem, f32[1,512]{1,0:T(1,128)S(1)} %get-tuple-element.13.gain_ref._, bf16[512,512]{1,0:T(8,128)(2,1)S(1)} %get-tuple-element.14.wq_ref, bf16[64,128,128]{2,1,0:T(8,128)(2,1)S(1)} %get-tuple-element.15.weight_ref, ...), custom_call_target="tpu_custom_call" | custom-call | flops 1048576 | bytes 65536 | tf_op jit(solution)/shard_map/own_tiles/pallas_call | solution.py:261
  39.9 2.4 %collective-permute-done.5.part_ref = bf16[512,512]{1,0:T(8,128)(2,1)S(1)} collective-permute-done((bf16[512,512]{1,0:T(8,128)(2,1)S(1)}, bf16[512,512]{1,0:T(8,128)(2,1)S(1)}, u32[]{:S(2)}, u32[]{:S(2)}) %collective-permute-start.5) | collective-permute-done | bytes 524320 | tf_op jit(solution)/shard_map/ppermute | solution.py:25
  42.4 0.2 add.3.sum_ref
  42.6 0.0 copy-start
  42.6 0.0 copy-start.1
  42.6 0.0 copy-start.2
  42.6 0.0 collective-permute-done.6.part_ref
  42.6 0.2 add.4.sum_ref
  42.8 0.0 collective-permute-done.7.part_ref
  42.8 0.2 add.5.sum_ref
  43.0 9.7 %collective-permute-done.8.part_ref = bf16[512,512]{1,0:T(8,128)(2,1)S(1)} collective-permute-done((bf16[512,512]{1,0:T(8,128)(2,1)S(1)}, bf16[512,512]{1,0:T(8,128)(2,1)S(1)}, u32[]{:S(2)}, u32[]{:S(2)}) %collective-permute-start.8) | collective-permute-done | bytes 524320 | tf_op jit(solution)/shard_map/ppermute | solution.py:25
  52.8 0.0 copy-done
  52.8 0.0 copy-done.1
  52.8 0.0 copy-done.2
  52.8 1.3 %mix.1 = bf16[512,512]{1,0:T(8,128)(2,1)} custom-call(bf16[512,512]{1,0:T(8,128)(2,1)S(1)} %copy-done, f32[1,512]{1,0:T(1,128)S(1)} %bitcast.3, bf16[512,512]{1,0:T(8,128)(2,1)S(1)} %copy-done.1, f32[512,512]{1,0:T(8,128)S(1)} %add.5.sum_ref, bf16[512,512]{1,0:T(8,128)(2,1)S(1)} %collective-permute-done.8.part_ref), custom_call_target="tpu_custom_call" | custom-call | flops 1048576 | bytes 65536 | tf_op jit(solution)/shard_map/mix/pallas_call | solution.py:292
Async XLA Ops:
  0.0 5.7 %collective-permute-start = (bf16[512,512]{1,0:T(8,128)(2,1)}, bf16[512,512]{1,0:T(8,128)(2,1)S(1)}, u32[]{:S(2)}, u32[]{:S(2)}) collective-permute-start(bf16[512,512]{1,0:T(8,128)(2,1)} %nodes_ref.1), channel_id=1, source_target_pairs={{0,1},{1,0},{2,3},{3,2},{4,5},{5,4},{6,7},{7,6},{8,9},{9,8},{10,11... | collective-permute-start | bytes 1572872 | tf_op jit(solution)/shard_map/ppermute | solution.py:234
  0.0 14.5 %collective-permute-start.4 = (bf16[512,512]{1,0:T(8,128)(2,1)}, bf16[512,512]{1,0:T(8,128)(2,1)S(1)}, u32[]{:S(2)}, u32[]{:S(2)}) collective-permute-start(bf16[512,512]{1,0:T(8,128)(2,1)} %nodes_ref.1), channel_id=1, source_target_pairs={{0,2},{4,6},{8,10},{12,14},{2,0},{6,4},{10,8},{14,12},{1,3},{5,7},... | collective-permute-start | bytes 1572872 | tf_op jit(solution)/shard_map/ppermute | solution.py:25
  1.5 16.9 %collective-permute-start.3 = (bf16[512,512]{1,0:T(8,128)(2,1)}, bf16[512,512]{1,0:T(8,128)(2,1)S(1)}, u32[]{:S(2)}, u32[]{:S(2)}) collective-permute-start(bf16[512,512]{1,0:T(8,128)(2,1)} %nodes_ref.1), channel_id=1, source_target_pairs={{4,8},{6,10},{8,4},{10,6},{5,9},{7,11},{9,5},{11,7},{20,24},{22,26... | collective-permute-start | bytes 1572872 | tf_op jit(solution)/shard_map/ppermute | solution.py:25
  5.0 20.0 %collective-permute-start.2 = (bf16[512,512]{1,0:T(8,128)(2,1)}, bf16[512,512]{1,0:T(8,128)(2,1)S(1)}, u32[]{:S(2)}, u32[]{:S(2)}) collective-permute-start(bf16[512,512]{1,0:T(8,128)(2,1)} %nodes_ref.1), channel_id=1, source_target_pairs={{0,4},{2,6},{8,12},{10,14},{4,0},{6,2},{12,8},{14,10},{1,5},{3,7},... | collective-permute-start | bytes 1572872 | tf_op jit(solution)/shard_map/ppermute | solution.py:25
  9.2 22.1 %collective-permute-start.1 = (bf16[512,512]{1,0:T(8,128)(2,1)S(1)}, bf16[512,512]{1,0:T(8,128)(2,1)S(1)}, u32[]{:S(2)}, u32[]{:S(2)}) collective-permute-start(bf16[512,512]{1,0:T(8,128)(2,1)S(1)} %get-tuple-element.18.block_ref), channel_id=1, source_target_pairs={{2,4},{6,8},{10,12},{4,2},{8,6},{12,10},{3,5},{7,9},{11,13},{5,3},... | collective-permute-start | bytes 1572872 | tf_op jit(solution)/shard_map/ppermute | solution.py:25
  16.1 26.2 %collective-permute-start.5 = (bf16[512,512]{1,0:T(8,128)(2,1)S(1)}, bf16[512,512]{1,0:T(8,128)(2,1)S(1)}, u32[]{:S(2)}, u32[]{:S(2)}) collective-permute-start(bf16[512,512]{1,0:T(8,128)(2,1)S(1)} %tiles_1_0.1._), channel_id=1, source_target_pairs={{0,2},{4,6},{8,10},{12,14},{2,0},{6,4},{10,8},{14,12},{1,3},{5,7},... | collective-permute-start | bytes 1572872 | tf_op jit(solution)/shard_map/ppermute | solution.py:25
  20.6 22.0 %collective-permute-start.6 = (bf16[512,512]{1,0:T(8,128)(2,1)S(1)}, bf16[512,512]{1,0:T(8,128)(2,1)S(1)}, u32[]{:S(2)}, u32[]{:S(2)}) collective-permute-start(bf16[512,512]{1,0:T(8,128)(2,1)S(1)} %tiles_2_1.1._), channel_id=1, source_target_pairs={{4,8},{6,10},{8,4},{10,6},{5,9},{7,11},{9,5},{11,7},{20,24},{22,26... | collective-permute-start | bytes 1572872 | tf_op jit(solution)/shard_map/ppermute | solution.py:25
  27.3 15.5 %collective-permute-start.7 = (bf16[512,512]{1,0:T(8,128)(2,1)S(1)}, bf16[512,512]{1,0:T(8,128)(2,1)S(1)}, u32[]{:S(2)}, u32[]{:S(2)}) collective-permute-start(bf16[512,512]{1,0:T(8,128)(2,1)S(1)} %tiles_2_0.1._), channel_id=1, source_target_pairs={{0,4},{2,6},{8,12},{10,14},{4,0},{6,2},{12,8},{14,10},{1,5},{3,7},... | collective-permute-start | bytes 1572872 | tf_op jit(solution)/shard_map/ppermute | solution.py:25
  33.0 19.7 %collective-permute-start.8 = (bf16[512,512]{1,0:T(8,128)(2,1)S(1)}, bf16[512,512]{1,0:T(8,128)(2,1)S(1)}, u32[]{:S(2)}, u32[]{:S(2)}) collective-permute-start(bf16[512,512]{1,0:T(8,128)(2,1)S(1)} %tiles_1_1.1._), channel_id=1, source_target_pairs={{2,4},{6,8},{10,12},{4,2},{8,6},{12,10},{3,5},{7,9},{11,13},{5,3},... | collective-permute-start | bytes 1572872 | tf_op jit(solution)/shard_map/ppermute | solution.py:25
  42.6 10.2 %copy-start = (bf16[512,512]{1,0:T(8,128)(2,1)S(1)}, bf16[512,512]{1,0:T(8,128)(2,1)}, u32[]{:S(2)}) copy-start(bf16[512,512]{1,0:T(8,128)(2,1)} %nodes_ref.1) | copy-start | bytes 1572868
  42.6 10.2 %copy-start.1 = (bf16[512,512]{1,0:T(8,128)(2,1)S(1)}, bf16[512,512]{1,0:T(8,128)(2,1)}, u32[]{:S(2)}) copy-start(bf16[512,512]{1,0:T(8,128)(2,1)} %w_out_ref.1) | copy-start | bytes 1572868
  42.6 10.2 %copy-start.2 = (f32[512]{0:T(512)S(1)}, f32[512]{0:T(512)}, u32[]{:S(2)}) copy-start(f32[512]{0:T(512)} %param.17) | copy-start | bytes 6148

commit v5 on v4

--- a/solution.py
+++ b/solution.py
@@ -116,6 +116,12 @@
     return copies
 
 
+def query_kernel(nodes_hbm, gain_hbm, wq_hbm, query_ref, nodes_ref, gain_ref, wq_ref, sems):
+    for copy in start_copies([(nodes_hbm, nodes_ref), (gain_hbm, gain_ref), (wq_hbm, wq_ref)], sems):
+        copy.wait()
+    query_ref[...] = scaled_query(rms_scale(nodes_ref[...], gain_ref[...]).astype(BF16), wq_ref)
+
+
 def make_lists(blocks, source, target, live, list_ref):
     codes, tiles = list_ref.shape[0] // 2, source.shape[1]
     square = (tiles, tiles)
@@ -232,7 +238,22 @@
     near, diagonal = (1, 0), (1, 1)
     places = (near, (HALO, 1), (HALO, 0), diagonal)
     other = lax.ppermute(nodes, "col", [(0, 1), (1, 0)])
-    arrived = {place: swap(nodes, "row", *place) for place in places if place != diagonal}
+    arrived = {near: swap(nodes, "row", *near)}
+    early = pl.pallas_call(
+        query_kernel,
+        out_shape=block_bf16,
+        in_specs=[HBM] * 3,
+        out_specs=VMEM,
+        scratch_shapes=[
+            pltpu.VMEM((rows_dev, features), BF16), pltpu.VMEM((1, features), F32), square,
+            pltpu.SemaphoreType.DMA((3,)),
+        ],
+        compiler_params=params,
+        cost_estimate=cost,
+        name="query",
+    )(*in_hbm(nodes, ln_gain.reshape(1, features), w_query))
+    for place in places[1:3]:
+        arrived[place] = swap(early, "row", *place)
 
     keys, values, weight_held, query, gain, wq, lists_out = pl.pallas_call(
         functools.partial(prepare_kernel, blocks),
@@ -274,7 +295,7 @@
 
     last, returned = gain, []
     for place in places:
-        last = tiles("tiles_%d_%d" % place, place, place == diagonal, arrived[place], last, block_bf16)
+        last = tiles("tiles_%d_%d" % place, place, place != near, arrived[place], last, block_bf16)
         returned.append(swap(last, "row", *place))
     total = tiles("own_tiles", None, True, query, last, block_f32)
     for part in returned[:-1]:

time: 54.3 us -> 55.9 us (1.029)
  Pallas kernels: 16.2 us -> 22.2 us
  starting transfers between devices: 18.9 us -> 15.8 us
  waiting for transfers between devices: 18.2 us -> 16.9 us
    pallas_call x5, Pallas kernels: 10.8 us -> 15 us  [tiles(): pl.pallas_call(functools.partial(tiles_kernel, place, projected), out_sha...]
    ppermute x8, starting transfers between devices: 18.9 us -> 15.8 us  [swap(): return lax.ppermute(block, axis, pairs + [(j, i) for i, j in pairs])]
    pallas_call x0 -> x1, Pallas kernels: none -> 1.76 us  [local(): pl.pallas_call(query_kernel, out_shape=block_bf16, in_specs=[HBM] * 3, ou...]
    ppermute x8, waiting for transfers between devices: 18.2 us -> 16.9 us  [swap(): return lax.ppermute(block, axis, pairs + [(j, i) for i, j in pairs])]
  transfers between devices with their start and end apart: 9 -> 9, of which waited for: 5 -> 4; matrix products, arithmetic and copies ran while one was open for 0% -> 0% of each run, Pallas kernels for 27% -> 37%
where the time goes in v5:
time: 55.9 us; the launch traced here: 55.7 us
  Pallas kernels  22.2 us (40%)
  waiting for transfers between devices  16.9 us (30%)
  starting transfers between devices  15.8 us (28%)
  between operations  0.84 us (2%)
    ppermute x8, waiting for transfers between devices, swap(): return lax.ppermute(block, axis, pairs + [(j, i) for i, j in pairs])  16.9 us
    ppermute x8, starting transfers between devices, swap(): return lax.ppermute(block, axis, pairs + [(j, i) for i, j in pairs])  15.8 us
    pallas_call x5, Pallas kernels, tiles(): pl.pallas_call(functools.partial(tiles_kernel, place, projected), out_sha...  15 us
    pallas_call x1, Pallas kernels, local(): pl.pallas_call(functools.partial(prepare_kernel, blocks), out_shape=(pack...  3.48 us
    pallas_call x1, Pallas kernels, local(): pl.pallas_call(query_kernel, out_shape=block_bf16, in_specs=[HBM] * 3, ou...  1.76 us
    pallas_call x1, Pallas kernels, local(): pl.pallas_call(last_kernel, out_shape=block_bf16, in_specs=[VMEM] * 5, ou...  1.34 us
  transfers between devices with their start and end apart: 9, of which 4 were waited for; matrix products, arithmetic and copies ran while one was open for 0% of the time, Pallas kernels for 37%

profile of v5, /device:TPU:8, one launch (start us, length us, event | category | flops | bytes accessed | tf_op | source)
XLA Modules:
  0.0 55.7 jit_solution(17063983311682438371)
XLA Ops:
  0.0 0.0 collective-permute-start
  0.0 1.5 %collective-permute-start.4 = (bf16[512,512]{1,0:T(8,128)(2,1)}, bf16[512,512]{1,0:T(8,128)(2,1)S(1)}, u32[]{:S(2)}, u32[]{:S(2)}) collective-permute-start(bf16[512,512]{1,0:T(8,128)(2,1)} %nodes_ref.1), channel_id=1, source_target_pairs={{0,2},{4,6},{8,10},{12,14},{2,0},{6,4},{10,8},{14,12},{1,3},{5,7},... | collective-permute-start | bytes 1572872 | tf_op jit(solution)/shard_map/ppermute | solution.py:25
  1.5 1.8 %query.1 = bf16[512,512]{1,0:T(8,128)(2,1)S(1)} custom-call(bf16[512,512]{1,0:T(8,128)(2,1)} %nodes_ref.1, f32[1,512]{1,0:T(1,128)} %bitcast.5, bf16[512,512]{1,0:T(8,128)(2,1)} %wq_hbm.3), custom_call_target="tpu_custom_call" | custom-call | flops 1048576 | bytes 65536 | tf_op jit(solution)/shard_map/query/pallas_call | solution.py:242
  3.3 3.5 %collective-permute-start.3 = (bf16[512,512]{1,0:T(8,128)(2,1)S(1)}, bf16[512,512]{1,0:T(8,128)(2,1)S(1)}, u32[]{:S(2)}, u32[]{:S(2)}) collective-permute-start(bf16[512,512]{1,0:T(8,128)(2,1)S(1)} %query.1), channel_id=1, source_target_pairs={{4,8},{6,10},{8,4},{10,6},{5,9},{7,11},{9,5},{11,7},{20,24},{22,26... | collective-permute-start | bytes 1572872 | tf_op jit(solution)/shard_map/ppermute | solution.py:25
  6.8 0.1 collective-permute-start.2
  7.5 0.0 collective-permute-done.other_ref
  7.5 3.5 %prepare.1 = (bf16[8,4,256,128]{3,2,1,0:T(8,128)(2,1)S(1)}, bf16[8,4,256,128]{3,2,1,0:T(8,128)(2,1)S(1)}, bf16[64,128,128]{2,1,0:T(8,128)(2,1)S(1)}, bf16[512,51...) custom-call(s32[1,64]{1,0:T(1,128)} %src_hbm.1, ...), custom_call_target="tpu_custom_call" | custom-call | flops 1048576 | bytes 65536 | tf_op jit(solution)/shard_map/prepare/pallas_call | solution.py:258
  11.0 3.9 %collective-permute-start.1 = (bf16[512,512]{1,0:T(8,128)(2,1)S(1)}, bf16[512,512]{1,0:T(8,128)(2,1)S(1)}, u32[]{:S(2)}, u32[]{:S(2)}) collective-permute-start(bf16[512,512]{1,0:T(8,128)(2,1)S(1)} %get-tuple-element.18.block_ref), channel_id=1, source_target_pairs={{2,4},{6,8},{10,12},{4,2},{8,6},{12,10},{3,5},{7,9},{11,13},{5,3},... | collective-permute-start | bytes 1572872 | tf_op jit(solution)/shard_map/ppermute | solution.py:25
  14.9 0.0 collective-permute-done.4.block_ref
  14.9 3.0 %tiles_1_0.1._ = bf16[512,512]{1,0:T(8,128)(2,1)S(1)} custom-call(s32[11,128]{1,0:T(8,128)S(1)} %get-tuple-element.12.lists_vmem, f32[1,512]{1,0:T(1,128)S(1)} %get-tuple-element.13.gain_ref._, bf16[512,512]{1,0:T(8,128)(2,1)S(1)} %get-tuple-element.14.wq_ref, bf16[64,128,128]{2,1,0:T(8,128)(2,1)S(1)} %get-tuple-element.15.weight_ref, ...), custom_call_target="tpu_custom_call" | custom-call | flops 1048576 | bytes 65536 | tf_op jit(solution)/shard_map/tiles_1_0/pallas_call | solution.py:282
  17.9 1.2 %collective-permute-start.5 = (bf16[512,512]{1,0:T(8,128)(2,1)S(1)}, bf16[512,512]{1,0:T(8,128)(2,1)S(1)}, u32[]{:S(2)}, u32[]{:S(2)}) collective-permute-start(bf16[512,512]{1,0:T(8,128)(2,1)S(1)} %tiles_1_0.1._), channel_id=1, source_target_pairs={{0,2},{4,6},{8,10},{12,14},{2,0},{6,4},{10,8},{14,12},{1,3},{5,7},... | collective-permute-start | bytes 1572872 | tf_op jit(solution)/shard_map/ppermute | solution.py:25
  19.1 0.8 %collective-permute-done.3.block_ref = bf16[512,512]{1,0:T(8,128)(2,1)S(1)} collective-permute-done((bf16[512,512]{1,0:T(8,128)(2,1)S(1)}, bf16[512,512]{1,0:T(8,128)(2,1)S(1)}, u32[]{:S(2)}, u32[]{:S(2)}) %collective-permute-start.3) | collective-permute-done | bytes 524320 | tf_op jit(solution)/shard_map/ppermute | solution.py:25
  19.9 3.0 %tiles_2_1.1._ = bf16[512,512]{1,0:T(8,128)(2,1)S(1)} custom-call(s32[11,128]{1,0:T(8,128)S(1)} %get-tuple-element.12.lists_vmem, f32[1,512]{1,0:T(1,128)S(1)} %get-tuple-element.13.gain_ref._, bf16[512,512]{1,0:T(8,128)(2,1)S(1)} %get-tuple-element.14.wq_ref, bf16[64,128,128]{2,1,0:T(8,128)(2,1)S(1)} %get-tuple-element.15.weight_ref, ...), custom_call_target="tpu_custom_call" | custom-call | flops 1048576 | bytes 65536 | tf_op jit(solution)/shard_map/tiles_2_1/pallas_call | solution.py:282
  22.9 3.5 %collective-permute-start.6 = (bf16[512,512]{1,0:T(8,128)(2,1)S(1)}, bf16[512,512]{1,0:T(8,128)(2,1)S(1)}, u32[]{:S(2)}, u32[]{:S(2)}) collective-permute-start(bf16[512,512]{1,0:T(8,128)(2,1)S(1)} %tiles_2_1.1._), channel_id=1, source_target_pairs={{4,8},{6,10},{8,4},{10,6},{5,9},{7,11},{9,5},{11,7},{20,24},{22,26... | collective-permute-start | bytes 1572872 | tf_op jit(solution)/shard_map/ppermute | solution.py:25
  26.4 0.0 collective-permute-done.2.block_ref
  26.4 2.9 %tiles_2_0.1._ = bf16[512,512]{1,0:T(8,128)(2,1)S(1)} custom-call(s32[11,128]{1,0:T(8,128)S(1)} %get-tuple-element.12.lists_vmem, f32[1,512]{1,0:T(1,128)S(1)} %get-tuple-element.13.gain_ref._, bf16[512,512]{1,0:T(8,128)(2,1)S(1)} %get-tuple-element.14.wq_ref, bf16[64,128,128]{2,1,0:T(8,128)(2,1)S(1)} %get-tuple-element.15.weight_ref, ...), custom_call_target="tpu_custom_call" | custom-call | flops 1048576 | bytes 65536 | tf_op jit(solution)/shard_map/tiles_2_0/pallas_call | solution.py:282
  29.3 0.1 collective-permute-start.7
  29.4 3.4 %collective-permute-done.1.block_ref = bf16[512,512]{1,0:T(8,128)(2,1)S(1)} collective-permute-done((bf16[512,512]{1,0:T(8,128)(2,1)S(1)}, bf16[512,512]{1,0:T(8,128)(2,1)S(1)}, u32[]{:S(2)}, u32[]{:S(2)}) %collective-permute-start.1) | collective-permute-done | bytes 524320 | tf_op jit(solution)/shard_map/ppermute | solution.py:25
  32.9 3.1 %tiles_1_1.1._ = bf16[512,512]{1,0:T(8,128)(2,1)S(1)} custom-call(s32[11,128]{1,0:T(8,128)S(1)} %get-tuple-element.12.lists_vmem, f32[1,512]{1,0:T(1,128)S(1)} %get-tuple-element.13.gain_ref._, bf16[512,512]{1,0:T(8,128)(2,1)S(1)} %get-tuple-element.14.wq_ref, bf16[64,128,128]{2,1,0:T(8,128)(2,1)S(1)} %get-tuple-element.15.weight_ref, ...), custom_call_target="tpu_custom_call" | custom-call | flops 1048576 | bytes 65536 | tf_op jit(solution)/shard_map/tiles_1_1/pallas_call | solution.py:282
  36.0 2.0 %collective-permute-start.8 = (bf16[512,512]{1,0:T(8,128)(2,1)S(1)}, bf16[512,512]{1,0:T(8,128)(2,1)S(1)}, u32[]{:S(2)}, u32[]{:S(2)}) collective-permute-start(bf16[512,512]{1,0:T(8,128)(2,1)S(1)} %tiles_1_1.1._), channel_id=1, source_target_pairs={{2,4},{6,8},{10,12},{4,2},{8,6},{12,10},{3,5},{7,9},{11,13},{5,3},... | collective-permute-start | bytes 1572872 | tf_op jit(solution)/shard_map/ppermute | solution.py:25
  38.0 3.0 %own_tiles.1.sum_ref = f32[512,512]{1,0:T(8,128)S(1)} custom-call(s32[11,128]{1,0:T(8,128)S(1)} %get-tuple-element.12.lists_vmem, f32[1,512]{1,0:T(1,128)S(1)} %get-tuple-element.13.gain_ref._, bf16[512,512]{1,0:T(8,128)(2,1)S(1)} %get-tuple-element.14.wq_ref, bf16[64,128,128]{2,1,0:T(8,128)(2,1)S(1)} %get-tuple-element.15.weight_ref, ...), custom_call_target="tpu_custom_call" | custom-call | flops 1048576 | bytes 65536 | tf_op jit(solution)/shard_map/own_tiles/pallas_call | solution.py:282
  41.0 1.4 %collective-permute-done.5.part_ref = bf16[512,512]{1,0:T(8,128)(2,1)S(1)} collective-permute-done((bf16[512,512]{1,0:T(8,128)(2,1)S(1)}, bf16[512,512]{1,0:T(8,128)(2,1)S(1)}, u32[]{:S(2)}, u32[]{:S(2)}) %collective-permute-start.5) | collective-permute-done | bytes 524320 | tf_op jit(solution)/shard_map/ppermute | solution.py:25
  42.4 0.2 add.3.sum_ref
  42.6 0.0 copy-start
  42.6 0.0 copy-start.1
  42.6 0.0 copy-start.2
  42.6 0.0 collective-permute-done.6.part_ref
  42.6 0.2 add.4.sum_ref
  42.8 0.0 collective-permute-done.7.part_ref
  42.8 0.2 add.5.sum_ref
  43.1 11.3 %collective-permute-done.8.part_ref = bf16[512,512]{1,0:T(8,128)(2,1)S(1)} collective-permute-done((bf16[512,512]{1,0:T(8,128)(2,1)S(1)}, bf16[512,512]{1,0:T(8,128)(2,1)S(1)}, u32[]{:S(2)}, u32[]{:S(2)}) %collective-permute-start.8) | collective-permute-done | bytes 524320 | tf_op jit(solution)/shard_map/ppermute | solution.py:25
  54.3 0.0 copy-done
  54.3 0.0 copy-done.1
  54.3 0.0 copy-done.2
  54.3 1.3 %mix.1 = bf16[512,512]{1,0:T(8,128)(2,1)} custom-call(bf16[512,512]{1,0:T(8,128)(2,1)S(1)} %copy-done, f32[1,512]{1,0:T(1,128)S(1)} %bitcast.3, bf16[512,512]{1,0:T(8,128)(2,1)S(1)} %copy-done.1, f32[512,512]{1,0:T(8,128)S(1)} %add.5.sum_ref, bf16[512,512]{1,0:T(8,128)(2,1)S(1)} %collective-permute-done.8.part_ref), custom_call_target="tpu_custom_call" | custom-call | flops 1048576 | bytes 65536 | tf_op jit(solution)/shard_map/mix/pallas_call | solution.py:313
Async XLA Ops:
  0.0 7.5 %collective-permute-start = (bf16[512,512]{1,0:T(8,128)(2,1)}, bf16[512,512]{1,0:T(8,128)(2,1)S(1)}, u32[]{:S(2)}, u32[]{:S(2)}) collective-permute-start(bf16[512,512]{1,0:T(8,128)(2,1)} %nodes_ref.1), channel_id=1, source_target_pairs={{0,1},{1,0},{2,3},{3,2},{4,5},{5,4},{6,7},{7,6},{8,9},{9,8},{10,11... | collective-permute-start | bytes 1572872 | tf_op jit(solution)/shard_map/ppermute | solution.py:240
  0.0 14.9 %collective-permute-start.4 = (bf16[512,512]{1,0:T(8,128)(2,1)}, bf16[512,512]{1,0:T(8,128)(2,1)S(1)}, u32[]{:S(2)}, u32[]{:S(2)}) collective-permute-start(bf16[512,512]{1,0:T(8,128)(2,1)} %nodes_ref.1), channel_id=1, source_target_pairs={{0,2},{4,6},{8,10},{12,14},{2,0},{6,4},{10,8},{14,12},{1,3},{5,7},... | collective-permute-start | bytes 1572872 | tf_op jit(solution)/shard_map/ppermute | solution.py:25
  3.3 16.7 %collective-permute-start.3 = (bf16[512,512]{1,0:T(8,128)(2,1)S(1)}, bf16[512,512]{1,0:T(8,128)(2,1)S(1)}, u32[]{:S(2)}, u32[]{:S(2)}) collective-permute-start(bf16[512,512]{1,0:T(8,128)(2,1)S(1)} %query.1), channel_id=1, source_target_pairs={{4,8},{6,10},{8,4},{10,6},{5,9},{7,11},{9,5},{11,7},{20,24},{22,26... | collective-permute-start | bytes 1572872 | tf_op jit(solution)/shard_map/ppermute | solution.py:25
  6.8 19.6 %collective-permute-start.2 = (bf16[512,512]{1,0:T(8,128)(2,1)S(1)}, bf16[512,512]{1,0:T(8,128)(2,1)S(1)}, u32[]{:S(2)}, u32[]{:S(2)}) collective-permute-start(bf16[512,512]{1,0:T(8,128)(2,1)S(1)} %query.1), channel_id=1, source_target_pairs={{0,4},{2,6},{8,12},{10,14},{4,0},{6,2},{12,8},{14,10},{1,5},{3,7},... | collective-permute-start | bytes 1572872 | tf_op jit(solution)/shard_map/ppermute | solution.py:25
  11.0 21.9 %collective-permute-start.1 = (bf16[512,512]{1,0:T(8,128)(2,1)S(1)}, bf16[512,512]{1,0:T(8,128)(2,1)S(1)}, u32[]{:S(2)}, u32[]{:S(2)}) collective-permute-start(bf16[512,512]{1,0:T(8,128)(2,1)S(1)} %get-tuple-element.18.block_ref), channel_id=1, source_target_pairs={{2,4},{6,8},{10,12},{4,2},{8,6},{12,10},{3,5},{7,9},{11,13},{5,3},... | collective-permute-start | bytes 1572872 | tf_op jit(solution)/shard_map/ppermute | solution.py:25
  17.9 24.5 %collective-permute-start.5 = (bf16[512,512]{1,0:T(8,128)(2,1)S(1)}, bf16[512,512]{1,0:T(8,128)(2,1)S(1)}, u32[]{:S(2)}, u32[]{:S(2)}) collective-permute-start(bf16[512,512]{1,0:T(8,128)(2,1)S(1)} %tiles_1_0.1._), channel_id=1, source_target_pairs={{0,2},{4,6},{8,10},{12,14},{2,0},{6,4},{10,8},{14,12},{1,3},{5,7},... | collective-permute-start | bytes 1572872 | tf_op jit(solution)/shard_map/ppermute | solution.py:25
  22.9 19.7 %collective-permute-start.6 = (bf16[512,512]{1,0:T(8,128)(2,1)S(1)}, bf16[512,512]{1,0:T(8,128)(2,1)S(1)}, u32[]{:S(2)}, u32[]{:S(2)}) collective-permute-start(bf16[512,512]{1,0:T(8,128)(2,1)S(1)} %tiles_2_1.1._), channel_id=1, source_target_pairs={{4,8},{6,10},{8,4},{10,6},{5,9},{7,11},{9,5},{11,7},{20,24},{22,26... | collective-permute-start | bytes 1572872 | tf_op jit(solution)/shard_map/ppermute | solution.py:25
  29.3 13.5 %collective-permute-start.7 = (bf16[512,512]{1,0:T(8,128)(2,1)S(1)}, bf16[512,512]{1,0:T(8,128)(2,1)S(1)}, u32[]{:S(2)}, u32[]{:S(2)}) collective-permute-start(bf16[512,512]{1,0:T(8,128)(2,1)S(1)} %tiles_2_0.1._), channel_id=1, source_target_pairs={{0,4},{2,6},{8,12},{10,14},{4,0},{6,2},{12,8},{14,10},{1,5},{3,7},... | collective-permute-start | bytes 1572872 | tf_op jit(solution)/shard_map/ppermute | solution.py:25
  36.0 18.3 %collective-permute-start.8 = (bf16[512,512]{1,0:T(8,128)(2,1)S(1)}, bf16[512,512]{1,0:T(8,128)(2,1)S(1)}, u32[]{:S(2)}, u32[]{:S(2)}) collective-permute-start(bf16[512,512]{1,0:T(8,128)(2,1)S(1)} %tiles_1_1.1._), channel_id=1, source_target_pairs={{2,4},{6,8},{10,12},{4,2},{8,6},{12,10},{3,5},{7,9},{11,13},{5,3},... | collective-permute-start | bytes 1572872 | tf_op jit(solution)/shard_map/ppermute | solution.py:25
  42.6 11.7 %copy-start = (bf16[512,512]{1,0:T(8,128)(2,1)S(1)}, bf16[512,512]{1,0:T(8,128)(2,1)}, u32[]{:S(2)}) copy-start(bf16[512,512]{1,0:T(8,128)(2,1)} %nodes_ref.1) | copy-start | bytes 1572868
  42.6 11.7 %copy-start.1 = (bf16[512,512]{1,0:T(8,128)(2,1)S(1)}, bf16[512,512]{1,0:T(8,128)(2,1)}, u32[]{:S(2)}) copy-start(bf16[512,512]{1,0:T(8,128)(2,1)} %w_out_ref.1) | copy-start | bytes 1572868
  42.6 11.7 %copy-start.2 = (f32[512]{0:T(512)S(1)}, f32[512]{0:T(512)}, u32[]{:S(2)}) copy-start(f32[512]{0:T(512)} %param.17) | copy-start | bytes 6148
